TPU v7x, 512 devices: a whole 4x4x16 slice. The times are simulated.
512 devices in a mesh: ch: 8 (over x, z_hi), ctx: 64 (over y, z_lo, core).
Axes of the slice: x: 4, y: 4, z: 16 (z_hi: 2, z_lo: 8; z = z_hi * 8 + z_lo), core: 2. Of those that a mesh axis runs over, the one named last changes fastest.
Arguments:
- signal: bfloat16 [16384, 8192], P('ctx', 'ch'), may hold values from -6 to 6
- gate: bfloat16 [16384, 8192], P('ctx', 'ch'), may hold values from -6 to 6
- filter_taps: bfloat16 [16384, 8192], P('ctx', 'ch'), may hold values from -0.21875 to 0.21875
- skip: bfloat16 [8192], P('ch'), may hold values from -4 to 4
- residual: bfloat16 [16384, 8192], P('ctx', 'ch'), may hold values from -70 to 70
- gain: bfloat16 [8192], P('ch'), may hold values from 0.5 to 1.5
Outputs:
- new_residual: bfloat16 [16384, 8192], P('ctx', 'ch')
- normed: bfloat16 [16384, 8192], P('ctx', 'ch')
All inputs are finite; a program needn't handle non-finite values.
Results may differ from a plain program's by a relative error of at most 0.0075.
Values may be sent and summed in bfloat16 or wider, within the bound.
No kernel may reach another device: no remote copies, remote signals or barrier semaphores. Data moves between devices by JAX's collectives and lax.ppermute only.
A program may use at most 64 MiB of HBM per device.

v0:
```python
import math

import jax
import jax.numpy as jnp
from jax import lax
from jax.sharding import PartitionSpec as P

D = 8192
PANELS = 3


HIGHEST = lax.Precision.HIGHEST


def spread(x, axis, root):
    mine = lax.axis_index(axis) == root
    return lax.psum(jnp.where(mine, x, jnp.zeros_like(x)), axis)


def shifted(x, axis, by):
    length = lax.axis_size(axis)
    return lax.ppermute(x, axis, [(i, (i + by) % length) for i in range(length)])


def tables(length):
    index = jnp.arange(length, dtype=jnp.int32)
    phase = index[:, None] * index[None, :] % (2 * length)
    angle = phase.astype(jnp.float32) * (math.pi / length)
    cosine = jnp.cos(angle)
    sine = jnp.sin(angle)
    forward = jnp.concatenate([cosine, -sine], axis=0)
    forward_high = forward.astype(jnp.bfloat16)
    forward_low = (forward - forward_high.astype(jnp.float32)).astype(jnp.bfloat16)
    scale = jnp.where(index == 0, 1.0, 2.0).astype(jnp.float32) / (2 * length)
    inverse = jnp.concatenate([cosine * scale[None, :], -sine * scale[None, :]], axis=1)
    alternate = (1 - 2 * (index % 2)).astype(jnp.float32)
    return ((forward_high, forward_low), inverse, alternate)


def spectrum(forward, alternate, block):
    length = block.shape[0]
    both = jnp.dot(forward[0], block, preferred_element_type=jnp.float32) + jnp.dot(
        forward[1], block, preferred_element_type=jnp.float32
    )
    return (
        both[:length],
        both[length:],
        jnp.dot(alternate.astype(jnp.bfloat16), block, preferred_element_type=jnp.float32),
    )


def add_spectra(first, second):
    return (first[0] + second[0], first[1] + second[1], first[2] + second[2])


def coefficients(panels, alternate, last_sign):
    flips = alternate[:, None]
    result = []
    for offset in range(len(panels) + 1):
        terms = []
        if offset < len(panels):
            terms.append(panels[offset])
        if offset > 0:
            earlier = panels[offset - 1]
            terms.append((flips * earlier[0], flips * earlier[1], last_sign * earlier[2]))
        total = terms[0]
        for other in terms[1:]:
            total = add_spectra(total, other)
        result.append(total)
    return result


def product(weight, values):
    return (
        weight[0] * values[0] - weight[1] * values[1],
        weight[0] * values[1] + weight[1] * values[0],
        weight[2] * values[2],
    )


def invert(inverse, alternate, totals):
    length = inverse.shape[0]
    stacked = jnp.concatenate([totals[0], totals[1]], axis=0)
    nyquist = (alternate / (2 * length))[:, None] * totals[2][None, :]
    return jnp.dot(inverse, stacked, precision=HIGHEST) + nyquist


def local(signal, gate, filter_taps, skip, residual, gain):
    length = signal.shape[0]
    forward, inverse, alternate = tables(length)
    last_sign = 1.0 - 2.0 * (length % 2)
    panels = []
    for owner in range(PANELS):
        piece = spread(filter_taps, "ctx", owner)
        panels.append(spectrum(forward, alternate, piece))
    weights = coefficients(panels, alternate, last_sign)
    current = signal
    totals = product(weights[0], spectrum(forward, alternate, current))
    for offset in range(1, PANELS + 1):
        current = shifted(current, "ctx", 1)
        totals = add_spectra(
            totals, product(weights[offset], spectrum(forward, alternate, current))
        )
    conv = invert(inverse, alternate, totals)
    mixed = gate.astype(jnp.float32) * (
        conv + skip.astype(jnp.float32)[None, :] * signal.astype(jnp.float32)
    )
    new_residual = (residual.astype(jnp.float32) + mixed).astype(jnp.bfloat16)
    widened_rows = lax.optimization_barrier(new_residual).astype(jnp.float32)
    squares = lax.psum(jnp.sum(widened_rows * widened_rows, axis=1), "ch")
    mean_square = squares / D
    normed = (
        widened_rows * lax.rsqrt(mean_square + 1e-05)[:, None] * gain.astype(jnp.float32)[None, :]
    ).astype(jnp.bfloat16)
    return (new_residual, normed)


def solution(mesh):
    placed = (P("ctx", "ch"), P("ctx", "ch"), P("ctx", "ch"), P("ch"), P("ctx", "ch"), P("ch"))
    return jax.shard_map(
        local,
        mesh=mesh,
        in_specs=placed,
        out_specs=(P("ctx", "ch"), P("ctx", "ch")),
        check_vma=False,
    )
```

profile of v0, /device:TPU:1, one launch (start us, length us, event | category | flops | bytes accessed | tf_op | source)
XLA Modules:
  0.0 908.3 jit_solution(15843803979595138571)
XLA Ops:
  7.2 4.9 collective-permute-start
  12.2 2.3 broadcast_select_fusion
  14.6 1.0 sine_negate_fusion
  15.9 1.8 broadcast_multiply_fusion.1
  17.7 0.4 fusion.41
  18.2 0.4 convolution_add_fusion.5
  18.6 4.3 collective-permute-start.1
  23.0 1.5 fusion.43
  24.5 1.2 fusion.50
  25.7 2.8 convolution_add_fusion.3
  28.5 8.6 collective-permute-done.1
  37.1 2.1 collective-permute-start.2
  39.2 0.4 fusion.45
  39.9 1.8 convolution_add_fusion.1
  41.6 15.4 %collective-permute-done.2 = bf16[256,1024]{1,0:T(8,128)(2,1)S(1)} collective-permute-done((bf16[256,1024]{1,0:T(8,128)(2,1)S(1)}, bf16[256,1024]{1,0:T(8,128)(2,1)S(1)}, u32[]{:S(2)}, u32[]{:S(2)}) %collective-permute-start.2) | collective-permute-done | bytes 524320 | tf_op jit(solution)/shard_map/ppermute | solution.py:22
  57.2 0.4 fusion.46
  57.6 1.8 convolution_add_fusion
  59.4 791.8 %all-reduce.3.cloned.1.call-done = (bf16[256,1024]{1,0:T(8,128)(2,1)}, bf16[256,1024]{1,0:T(8,128)(2,1)}, bf16[256,1024]{1,0:T(8,128)(2,1)}) async-done(((bf16[256,1024]{1,0:T(8,128)(2,1)}, bf16[256,1024]{1,0:T(8,128)(2,1)}, bf16[256,1024]{1,0:T(8,128)(2,1)}), (bf16[256,1024]{1,0:T(8,128)(2,1)}, bf16[256,1024]{1,0:T(8,128)(2,1)}, bf16[256,1024]{1,0:T(8,128)(2,1)})) %all-reduce.3.cloned.1.call-update) | async-done | bytes 1572880 | tf_op jit(solution)/shard_map/psum | solution.py:17
  851.2 1.3 fusion.49
  852.5 1.5 fusion.42
  854.2 0.4 fusion.40
  855.2 0.4 fusion.44
  856.2 0.4 convolution_add_fusion.6
  856.6 0.4 convolution_add_fusion.2
  857.1 0.7 copy-done.2
  857.8 0.7 copy-done
  858.5 0.6 copy-done.1
  859.1 1.9 subtract_add_fusion
  861.1 1.9 add_add_fusion
  863.1 2.1 fusion.16
  865.3 35.1 %psum.31 = f32[256]{0:T(256)S(1)} all-reduce(f32[256]{0:T(256)S(1)} %fusion.19), channel_id=1, replica_groups=mesh['ch'=8,'ctx'=64] {'ch'}, use_global_device_ids=true, to_apply=%region_4.5 | all-reduce | flops 256 | bytes 2048 | tf_op jit(solution)/shard_map/psum | solution.py:110
  900.5 1.0 fusion.21
  (43 shorter events, 2.2 us)
Async XLA Ops:
  7.2 844.1 %all-reduce.3.cloned.1.call-start = ((), (), s32[]{:S(2)}) async-start(), calls=%async_computation | async-start | bytes 3145728 | tf_op jit(solution)/shard_map/psum | solution.py:17
  7.2 11.4 %collective-permute-start = (bf16[256,1024]{1,0:T(8,128)(2,1)}, bf16[256,1024]{1,0:T(8,128)(2,1)}, u32[]{:S(2)}, u32[]{:S(2)}) collective-permute-start(bf16[256,1024]{1,0:T(8,128)(2,1)} %param.6), channel_id=1, source_target_pairs={{0,1},{1,2},{2,3},{3,4},{4,5},{5,6},{6,7},{7,8},{8,9},{9,10},{10,1... | collective-permute-start | bytes 1572872 | tf_op jit(solution)/shard_map/ppermute | solution.py:22
  12.2 3.5 copy-start.3
  12.2 3.7 copy-start.9
  12.2 3.7 copy-start.10
  18.6 18.5 %collective-permute-start.1 = (bf16[256,1024]{1,0:T(8,128)(2,1)}, bf16[256,1024]{1,0:T(8,128)(2,1)S(1)}, u32[]{:S(2)}, u32[]{:S(2)}) collective-permute-start(bf16[256,1024]{1,0:T(8,128)(2,1)} %collective-permute-done), channel_id=1, source_target_pairs={{0,1},{1,2},{2,3},{3,4},{4,5},{5,6},{6,7},{7,8},{8,9},{9,10},{10,1... | collective-permute-start | bytes 1572872 | tf_op jit(solution)/shard_map/ppermute | solution.py:22
  37.1 19.8 %collective-permute-start.2 = (bf16[256,1024]{1,0:T(8,128)(2,1)S(1)}, bf16[256,1024]{1,0:T(8,128)(2,1)S(1)}, u32[]{:S(2)}, u32[]{:S(2)}) collective-permute-start(bf16[256,1024]{1,0:T(8,128)(2,1)S(1)} %collective-permute-done.1), channel_id=1, source_target_pairs={{0,1},{1,2},{2,3},{3,4},{4,5},{5,6},{6,7},{7,8},{8,9},{9,10},{10,1... | collective-permute-start | bytes 1572872 | tf_op jit(solution)/shard_map/ppermute | solution.py:22
  851.2 2.8 copy-start.5
  854.0 1.0 copy-start.4
  854.6 1.1 copy-start.6
  856.2 1.6 copy-start.2
  856.6 1.9 copy-start
  856.6 2.5 copy-start.1
  861.1 2.0 copy-start.8
  861.1 2.0 copy-start.11
  861.1 2.0 copy-start.12
  865.1 36.3 %copy-start.7 = (bf16[256,1024]{1,0:T(8,128)(2,1)}, bf16[256,1024]{1,0:T(8,128)(2,1)S(1)}, u32[]{:S(2)}) copy-start(bf16[256,1024]{1,0:T(8,128)(2,1)S(1)} %fusion.16) | copy-start | bytes 1572868
Sparse Core Ops, SparseCore 0:
  14.7 836.5 all-reduce.2
where the time goes:
time: 917 us; the launch traced here: 908 us
  waiting for transfers between devices  816 us (89%)
  blocking collectives  35.1 us (4%)
  matrix products  18.8 us (2%)
  between operations  14.4 us (2%)
  starting transfers between devices  11.4 us (1%)
  other arithmetic  10.3 us (1%)
    psum x1, waiting for transfers between devices, spread(): return lax.psum(jnp.where(mine, x, jnp.zeros_like(x)), axis)  792 us
    psum x1, blocking collectives, local(): squares = lax.psum(jnp.sum(widened_rows * widened_rows, axis=1), 'ch')  35.1 us
    ppermute x3, waiting for transfers between devices, shifted(): lax.ppermute(x, axis, [(i, (i + by) % length) for i in range(length)])  24 us
  transfers between devices with their start and end apart: 4, of which 3 were waited for; matrix products, arithmetic and copies ran while one was open for 2% of the time, Pallas kernels for 0%

commit v1 on v0

v1 whole, which is shorter than its diff:
```python
import functools
import math

import jax
import jax.numpy as jnp
import ml_dtypes
import numpy as np
from jax import lax
from jax.experimental import pallas as pl
from jax.experimental.pallas import tpu as pltpu
from jax.sharding import PartitionSpec as P

D = 8192
BLOCK = 256
PANELS = 3
HALF = 512
QUARTER = 128
LAGS = PANELS * BLOCK
WINDOW = LAGS + 2 * BLOCK
BINS = WINDOW // 2
TILE = 128
EPS = 1e-05
Y, Z, CORES = 4, 8, 2


def split(values):
    high = values.astype(np.float32).astype(ml_dtypes.bfloat16)
    low = (values - high.astype(np.float64)).astype(np.float32).astype(ml_dtypes.bfloat16)
    return high, low


@functools.cache
def tables():
    bins = np.arange(BINS)[:, None]
    points = np.arange(WINDOW)[None, :]
    angle = (bins * points % WINDOW) * (2 * math.pi / WINDOW)
    sign = (1.0 - 2.0 * (points % 2))[0]
    real = np.cos(angle)
    imag = -np.sin(angle)
    imag[0] = sign
    forward = np.concatenate([real, imag], axis=0)
    scale = np.where(np.arange(BINS) == 0, 1.0, 2.0)[:, None] / WINDOW
    back = np.concatenate([real * scale, imag * scale], axis=0).T[LAGS:]
    return split(forward), split(back)


def pairs(rule):
    result = []
    for index in range(Y * Z * CORES):
        target = rule(index // (Z * CORES), index // CORES % Z, index % CORES)
        if target is not None:
            y, z, core = target
            result.append((index, y % Y * Z * CORES + z * CORES + core))
    return result


def move(x, rule):
    return lax.ppermute(x, "ctx", pairs(rule))


def dot(a, b):
    return jnp.dot(a, b, preferred_element_type=jnp.float32)


def spectrum_kernel(high, low, x, out):
    for tile in range(WINDOW // BLOCK):
        rows = slice(tile * BLOCK, (tile + 1) * BLOCK)
        out[rows, :] = dot(high[rows, :], x[...]) + dot(low[rows, :], x[...])


def spectrum(high, low, x):
    return pl.pallas_call(
        spectrum_kernel,
        out_shape=jax.ShapeDtypeStruct((WINDOW, HALF), jnp.float32),
        in_specs=[pl.BlockSpec(memory_space=pltpu.VMEM)] * 3,
        out_specs=pl.BlockSpec(memory_space=pltpu.VMEM),
        compiler_params=pltpu.CompilerParams(vmem_limit_bytes=24 * 2**20),
        cost_estimate=pl.CostEstimate(
            flops=4 * WINDOW * WINDOW * HALF,
            bytes_accessed=4 * WINDOW * WINDOW + 6 * WINDOW * HALF,
            transcendentals=0,
        ),
    )(high, low, x)


def mix_kernel(
    core, high, low, back, taps, spec, signal, gate, residual, skip, kept, sent, sums, prod
):
    filt = jnp.concatenate([taps[q] for q in range(Y)], axis=1)
    for tile in range(BINS // TILE):
        real = slice(tile * TILE, (tile + 1) * TILE)
        imag = slice(BINS + tile * TILE, BINS + (tile + 1) * TILE)
        fr = dot(high[real, :], filt) + dot(low[real, :], filt)
        fi = dot(high[imag, :], filt) + dot(low[imag, :], filt)
        sr = spec[real, :]
        si = spec[imag, :]
        cross = si * fi
        pr = sr * fr - cross
        pi = sr * fi + si * fr
        if tile == 0:
            first = lax.broadcasted_iota(jnp.int32, (TILE, HALF), 0) == 0
            pr = jnp.where(first, sr * fr, pr)
            pi = jnp.where(first, cross, pi)
        prod[real, :] = pr.astype(jnp.bfloat16)
        prod[imag, :] = pi.astype(jnp.bfloat16)
    for block in range(2):
        rows = slice(block * BLOCK, (block + 1) * BLOCK)
        conv = dot(back[rows, :], prod[...])
        x = signal[rows, :].astype(jnp.float32)
        weight = skip[...].astype(jnp.float32)
        mixed = gate[rows, :].astype(jnp.float32) * (conv + weight * x)
        updated = (residual[rows, :].astype(jnp.float32) + mixed).astype(jnp.bfloat16)
        wide = updated.astype(jnp.float32)
        total = jnp.sum(wide * wide, axis=1)
        for other in range(8):
            sums[2 * other + block, :] = total

        @pl.when(core[0] == block)
        def _():
            kept[...] = updated

        @pl.when(core[0] != block)
        def _():
            sent[...] = updated


def mix(core, high, low, back, taps, spec, signal, gate, residual, skip):
    vmem = pl.BlockSpec(memory_space=pltpu.VMEM)
    return pl.pallas_call(
        mix_kernel,
        out_shape=(
            jax.ShapeDtypeStruct((BLOCK, HALF), jnp.bfloat16),
            jax.ShapeDtypeStruct((BLOCK, HALF), jnp.bfloat16),
            jax.ShapeDtypeStruct((16, BLOCK), jnp.float32),
        ),
        in_specs=[pl.BlockSpec(memory_space=pltpu.SMEM)] + [vmem] * 9,
        out_specs=(vmem, vmem, vmem),
        scratch_shapes=[pltpu.VMEM((WINDOW, HALF), jnp.bfloat16)],
        compiler_params=pltpu.CompilerParams(vmem_limit_bytes=24 * 2**20),
        cost_estimate=pl.CostEstimate(
            flops=4 * WINDOW * LAGS * HALF + 2 * WINDOW * 2 * BLOCK * HALF,
            bytes_accessed=4 * WINDOW * LAGS + 4 * WINDOW * HALF,
            transcendentals=0,
        ),
    )(core, high, low, back, taps, spec, signal, gate, residual, skip)


def local(signal, gate, filter_taps, skip, residual, gain):
    (high, low), (back, _) = tables()
    index = lax.axis_index("ctx")
    y, z, core = index // (Z * CORES), index // CORES % Z, index % CORES
    lead = core == 0

    def mine(x):
        return lax.dynamic_slice_in_dim(x, core * HALF, HALF, axis=1)

    def others(x):
        return lax.dynamic_slice_in_dim(x, (1 - core) * HALF, HALF, axis=1)

    def ordered(own, other):
        return jnp.concatenate([jnp.where(lead, own, other), jnp.where(lead, other, own)], axis=0)

    def swap(x):
        return move(others(x), lambda y, z, c: (y, z, 1 - c))

    def halves(x):
        return ordered(mine(x), swap(x))

    taps_other = move(
        others(filter_taps), lambda y, z, c: (y, z, 1 - c) if y == 0 and z < 2 else None
    )
    current = halves(signal)
    held = ordered(mine(filter_taps), taps_other)
    piece = [held[:, q * QUARTER : (q + 1) * QUARTER] for q in range(Y)]
    parts = [
        move(piece[q], lambda y, z, c, q=q: (q, z, c) if y == 0 and z < 2 else None)
        for q in (2, 1, 3)
    ]
    earlier = move(current, lambda y, z, c: (y, z + 1, c) if z < Z - 1 else (y + 1, 0, c))
    held = jnp.where(y == 0, piece[0], parts[0] + parts[1] + parts[2])
    got = move(held, lambda y, z, c: (y, z + 4, c) if z < 2 else None)
    held = jnp.where(z < 4, held, got)
    got = move(held, lambda y, z, c: (y, z + 2, c) if z % 4 < 2 else None)
    held = jnp.where(z % 4 < 2, held, got)
    first = move(
        earlier[BLOCK:], lambda y, z, c: (y, z + 1, c) if z < Z - 1 else (y + 1, 0, c)
    )
    got = move(held, lambda y, z, c: (y, z ^ 1, c))
    even = z % 2 == 0
    quarter = jnp.concatenate(
        [jnp.where(even, held, got), jnp.where(even, got, held)[:BLOCK]], axis=0
    )
    gates = halves(gate)
    residuals = halves(residual)
    spec = spectrum(high, low, jnp.concatenate([first, earlier, current], axis=0))
    groups = [[(a * Z + b) * CORES + c for a in range(Y)] for b in range(Z) for c in range(CORES)]
    taps = lax.all_gather(quarter, "ctx", axis_index_groups=groups)
    skips = lax.dynamic_slice_in_dim(skip, core * HALF, HALF)[None, :]
    kept, sent, sums = mix(
        core.astype(jnp.int32)[None],
        high[:, :LAGS],
        low[:, :LAGS],
        back,
        taps,
        spec,
        current,
        gates,
        residuals,
        skips,
    )
    received = move(sent, lambda y, z, c: (y, z, 1 - c))
    size = Y * Z * CORES
    groups = [
        [a * size + b * CORES + c for a in range(8) for c in range(CORES)] for b in range(Y * Z)
    ]
    squares = jnp.sum(
        lax.all_to_all(sums, ("ch", "ctx"), 0, 0, axis_index_groups=groups), axis=0
    )
    new_residual = jnp.concatenate(
        [jnp.where(lead, kept, received), jnp.where(lead, received, kept)], axis=1
    )
    scale = lax.rsqrt(squares / D + EPS)[:, None]
    normed = new_residual.astype(jnp.float32) * scale * gain.astype(jnp.float32)[None, :]
    return (new_residual, normed.astype(jnp.bfloat16))


def solution(mesh):
    placed = (P("ctx", "ch"), P("ctx", "ch"), P("ctx", "ch"), P("ch"), P("ctx", "ch"), P("ch"))
    return jax.shard_map(
        local,
        mesh=mesh,
        in_specs=placed,
        out_specs=(P("ctx", "ch"), P("ctx", "ch")),
        check_vma=False,
    )
```

time: 917 us -> 116 us (0.13)
  waiting for transfers between devices: 816 us -> 25.6 us
  starting transfers between devices: 11.4 us -> 54.9 us
  matrix products: 18.8 us -> 0 us
  blocking collectives: 35.1 us -> 18.3 us
  between operations: 14.4 us -> 1.16 us
    psum x1 -> x0, waiting for transfers between devices: 792 us -> none  [spread(): return lax.psum(jnp.where(mine, x, jnp.zeros_like(x)), axis)]
    psum x1 -> x0, blocking collectives: 35.1 us -> none  [local(): squares = lax.psum(jnp.sum(widened_rows * widened_rows, axis=1), 'ch')]
    ppermute x3 -> x13, starting transfers between devices: 11.4 us -> 38.6 us  [move(): return lax.ppermute(x, 'ctx', pairs(rule))]
    dot_general x22 -> x0, matrix products: 18.8 us -> none  [the longest x7 9.19 us: spectrum(): jnp.dot(forward[0], block, preferred_element_type=jnp.float32)]
    all_gather x0 -> x1, blocking collectives: none -> 18.3 us  [local(): taps = lax.all_gather(quarter, 'ctx', axis_index_groups=groups)]
    all_to_all x0 -> x1, starting transfers between devices: none -> 16.3 us  [local(): lax.all_to_all(sums, ('ch', 'ctx'), 0, 0, axis_index_groups=groups)]
    all_to_all x0 -> x1, waiting for transfers between devices: none -> 12.5 us  [local(): lax.all_to_all(sums, ('ch', 'ctx'), 0, 0, axis_index_groups=groups)]
    ppermute x3 -> x13, waiting for transfers between devices: 24 us -> 13.1 us  [move(): return lax.ppermute(x, 'ctx', pairs(rule))]
  transfers between devices with their start and end apart: 4 -> 14, of which waited for: 3 -> 3; matrix products, arithmetic and copies ran while one was open for 2% -> 4% of each run, Pallas kernels for 0% -> 0%
where the time goes in v1:
time: 116 us; the launch traced here: 115 us
  starting transfers between devices  54.9 us (47%)
  waiting for transfers between devices  25.6 us (22%)
  blocking collectives  18.3 us (16%)
  Pallas kernels  7.49 us (6%)
  other arithmetic  4.83 us (4%)
  local copies, waits for them, and re-layouts  2.89 us (2%)
  between operations  1.16 us (1%)
    ppermute x13, starting transfers between devices, move(): return lax.ppermute(x, 'ctx', pairs(rule))  38.6 us
    all_gather x1, blocking collectives, local(): taps = lax.all_gather(quarter, 'ctx', axis_index_groups=groups)  18.3 us
    all_to_all x1, starting transfers between devices, local(): lax.all_to_all(sums, ('ch', 'ctx'), 0, 0, axis_index_groups=groups)  16.3 us
    ppermute x13, waiting for transfers between devices, move(): return lax.ppermute(x, 'ctx', pairs(rule))  13.1 us
    all_to_all x1, waiting for transfers between devices, local(): lax.all_to_all(sums, ('ch', 'ctx'), 0, 0, axis_index_groups=groups)  12.5 us
    pallas_call x1, Pallas kernels, mix(): pl.pallas_call(mix_kernel, out_shape=(jax.ShapeDtypeStruct((BLOCK, HALF),...  3.95 us
    pallas_call x1, Pallas kernels, spectrum(): pl.pallas_call(spectrum_kernel, out_shape=jax.ShapeDtypeStruct((WINDOW, H...  3.53 us
  transfers between devices with their start and end apart: 14, of which 3 were waited for; matrix products, arithmetic and copies ran while one was open for 4% of the time, Pallas kernels for 0%

profile of v1, /device:TPU:1, one launch (start us, length us, event | category | flops | bytes accessed | tf_op | source)
XLA Modules:
  0.0 115.2 jit_solution(16141943788434209822)
XLA Ops:
  0.7 1.1 constant_dynamic-slice_fusion.3
  1.8 8.8 %collective-permute-start = (bf16[256,512]{1,0:T(8,128)(2,1)S(1)}, bf16[256,512]{1,0:T(8,128)(2,1)S(1)}, u32[]{:S(2)}, u32[]{:S(2)}) collective-permute-start(bf16[256,512]{1,0:T(8,128)(2,1)S(1)} %constant_dynamic-slice_fusion.3), channel_id=1, source_target_pairs={{0,1},{1,0},{2,3},{3,2},{64,65},{65,64},{66,67},{67,66},{128,129},... | collective-permute-start | bytes 786440 | tf_op jit(solution)/shard_map/ppermute | solution.py:58
  10.6 1.0 constant_dynamic-slice_fusion.2
  11.5 1.9 %collective-permute-start.7 = (bf16[256,512]{1,0:T(8,128)(2,1)S(1)}, bf16[256,512]{1,0:T(8,128)(2,1)S(1)}, u32[]{:S(2)}, u32[]{:S(2)}) collective-permute-start(bf16[256,512]{1,0:T(8,128)(2,1)S(1)} %constant_dynamic-slice_fusion.2), channel_id=1, source_target_pairs={{0,1},{1,0},{2,3},{3,2},{4,5},{5,4},{6,7},{7,6},{8,9},{9,8},{10,11... | collective-permute-start | bytes 786440 | tf_op jit(solution)/shard_map/ppermute | solution.py:58
  13.5 1.0 broadcast_select_fusion.8
  14.5 0.8 fusion
  15.3 1.9 %collective-permute-start.1 = (bf16[512,128]{1,0:T(8,128)(2,1)}, bf16[512,128]{1,0:T(8,128)(2,1)}, u32[]{:S(2)}, u32[]{:S(2)}) collective-permute-start(bf16[512,128]{1,0:T(8,128)(2,1)} %get-tuple-element.21), channel_id=1, source_target_pairs={{0,32},{1,33},{2,34},{3,35},{64,96},{65,97},{66,98},{67,99},{128,1... | collective-permute-start | bytes 393224 | tf_op jit(solution)/shard_map/ppermute | solution.py:58
  17.2 1.9 %collective-permute-start.2 = (bf16[512,128]{1,0:T(8,128)(2,1)}, bf16[512,128]{1,0:T(8,128)(2,1)}, u32[]{:S(2)}, u32[]{:S(2)}) collective-permute-start(bf16[512,128]{1,0:T(8,128)(2,1)} %get-tuple-element.20), channel_id=1, source_target_pairs={{0,16},{1,17},{2,18},{3,19},{64,80},{65,81},{66,82},{67,83},{128,1... | collective-permute-start | bytes 393224 | tf_op jit(solution)/shard_map/ppermute | solution.py:58
  19.2 1.9 %collective-permute-start.3 = (bf16[512,128]{1,0:T(8,128)(2,1)S(1)}, bf16[512,128]{1,0:T(8,128)(2,1)}, u32[]{:S(2)}, u32[]{:S(2)}) collective-permute-start(bf16[512,128]{1,0:T(8,128)(2,1)S(1)} %get-tuple-element.22), channel_id=1, source_target_pairs={{0,48},{1,49},{2,50},{3,51},{64,112},{65,113},{66,114},{67,115},{1... | collective-permute-start | bytes 393224 | tf_op jit(solution)/shard_map/ppermute | solution.py:58
  21.1 2.4 %collective-permute-start.10 = (bf16[256,512]{1,0:T(8,128)(2,1)S(1)}, bf16[256,512]{1,0:T(8,128)(2,1)S(1)}, u32[]{:S(2)}, u32[]{:S(2)}) collective-permute-start(bf16[256,512]{1,0:T(8,128)(2,1)S(1)} %constant_dynamic-slice_fusion.1), channel_id=1, source_target_pairs={{0,1},{1,0},{2,3},{3,2},{4,5},{5,4},{6,7},{7,6},{8,9},{9,8},{10,11... | collective-permute-start | bytes 786440 | tf_op jit(solution)/shard_map/ppermute | solution.py:58
  23.7 0.1 dynamic_slice.35
  23.8 1.9 %collective-permute-start.11 = (bf16[256,512]{1,0:T(8,128)(2,1)S(1)}, bf16[256,512]{1,0:T(8,128)(2,1)S(1)}, u32[]{:S(2)}, u32[]{:S(2)}) collective-permute-start(bf16[256,512]{1,0:T(8,128)(2,1)S(1)} %constant_dynamic-slice_fusion), channel_id=1, source_target_pairs={{0,1},{1,0},{2,3},{3,2},{4,5},{5,4},{6,7},{7,6},{8,9},{9,8},{10,11... | collective-permute-start | bytes 786440 | tf_op jit(solution)/shard_map/ppermute | solution.py:58
  25.7 1.1 fusion.2
  26.8 1.3 %collective-permute-start.4 = (bf16[512,128]{1,0:T(8,128)(2,1)S(1)}, bf16[512,128]{1,0:T(8,128)(2,1)S(1)}, u32[]{:S(2)}, u32[]{:S(2)}) collective-permute-start(bf16[512,128]{1,0:T(8,128)(2,1)S(1)} %fusion.2), channel_id=1, source_target_pairs={{0,8},{1,9},{2,10},{3,11},{16,24},{17,25},{18,26},{19,27},{32,40},... | collective-permute-start | bytes 393224 | tf_op jit(solution)/shard_map/ppermute | solution.py:58
  28.1 0.1 broadcast_select_fusion.7
  28.3 2.6 %collective-permute-start.8 = (bf16[512,512]{1,0:T(8,128)(2,1)S(1)}, bf16[512,512]{1,0:T(8,128)(2,1)S(1)}, u32[]{:S(2)}, u32[]{:S(2)}) collective-permute-start(bf16[512,512]{1,0:T(8,128)(2,1)S(1)} %pad_maximum_fusion.1.signal), channel_id=1, source_target_pairs={{0,2},{1,3},{2,4},{3,5},{4,6},{5,7},{6,8},{7,9},{8,10},{9,11},{10,... | collective-permute-start | bytes 1572872 | tf_op jit(solution)/shard_map/ppermute | solution.py:58
  30.9 1.3 %collective-permute-start.5 = (bf16[512,128]{1,0:T(8,128)(2,1)S(1)}, bf16[512,128]{1,0:T(8,128)(2,1)S(1)}, u32[]{:S(2)}, u32[]{:S(2)}) collective-permute-start(bf16[512,128]{1,0:T(8,128)(2,1)S(1)} %broadcast_select_fusion.10), channel_id=1, source_target_pairs={{0,4},{1,5},{2,6},{3,7},{8,12},{9,13},{10,14},{11,15},{16,20},{17,... | collective-permute-start | bytes 393224 | tf_op jit(solution)/shard_map/ppermute | solution.py:58
  32.3 0.3 broadcast_select_fusion.3
  32.5 12.5 %collective-permute-done.5 = bf16[512,128]{1,0:T(8,128)(2,1)S(1)} collective-permute-done((bf16[512,128]{1,0:T(8,128)(2,1)S(1)}, bf16[512,128]{1,0:T(8,128)(2,1)S(1)}, u32[]{:S(2)}, u32[]{:S(2)}) %collective-permute-start.5) | collective-permute-done | bytes 131104 | tf_op jit(solution)/shard_map/ppermute | solution.py:58
  45.0 8.3 %collective-permute-start.6 = (bf16[512,128]{1,0:T(8,128)(2,1)S(1)}, bf16[512,128]{1,0:T(8,128)(2,1)S(1)}, u32[]{:S(2)}, u32[]{:S(2)}) collective-permute-start(bf16[512,128]{1,0:T(8,128)(2,1)S(1)} %broadcast_select_fusion.11), channel_id=1, source_target_pairs={{0,2},{1,3},{2,0},{3,1},{4,6},{5,7},{6,4},{7,5},{8,10},{9,11},{10,... | collective-permute-start | bytes 393224 | tf_op jit(solution)/shard_map/ppermute | solution.py:58
  53.4 0.0 copy-start.3
  53.5 2.3 %collective-permute-start.9 = (bf16[256,512]{1,0:T(8,128)(2,1)S(1)}, bf16[256,512]{1,0:T(8,128)(2,1)S(1)}, u32[]{:S(2)}, u32[]{:S(2)}) collective-permute-start(bf16[256,512]{1,0:T(8,128)(2,1)S(1)} %slice.32), channel_id=1, source_target_pairs={{0,2},{1,3},{2,4},{3,5},{4,6},{5,7},{6,8},{7,9},{8,10},{9,11},{10,... | collective-permute-start | bytes 786440 | tf_op jit(solution)/shard_map/ppermute | solution.py:58
  55.8 0.6 collective-permute-done.6
  56.4 18.3 %all-gather = bf16[3072,128]{1,0:T(8,128)(2,1)S(1)} all-gather(bf16[768,128]{1,0:T(8,128)(2,1)S(1)} %pad_maximum_fusion.5), channel_id=2, replica_groups={{0,16,32,48},{1,17,33,49},{2,18,34,50},{3,19,35,51},{4,20,36,52},{5,21,..., dimensions={0}, use_global_device_ids=true | all-gather | bytes 983040 | tf_op jit(solution)/shard_map/all_gather | solution.py:197
  74.8 0.1 pad_maximum_fusion.x
  74.9 3.5 %shard_map.122.spec = f32[1280,512]{1,0:T(8,128)S(1)} custom-call(bf16[1280,1280]{1,0:T(8,128)(2,1)S(1)} %copy-done.3, bf16[1280,1280]{1,0:T(8,128)(2,1)S(1)} %copy-done.4, bf16[1280,512]{1,0:T(8,128)(2,1)S(1)} %pad_maximum_fusion.x), custom_call_target="tpu_custom_call" | custom-call | flops 3355443200 | bytes 10485760 | tf_op jit(solution)/shard_map/pallas_call | solution.py:72
  78.5 4.0 %shard_map.123 = (bf16[256,512]{1,0:T(8,128)(2,1)S(1)}, bf16[256,512]{1,0:T(8,128)(2,1)S(1)}, f32[16,256]{1,0:T(8,128)S(1)}) custom-call(s32[1]{0:T(128)} %bitcast.core, bf16[1280,768]{1,0:T(8,128)(2,1)S(1)} %copy-done, bf16[1280,768]{1,0:T(8,128)(2,1)S(1)} %copy-done.1, bf16[512,1280]{1,0:T(8,128)(2,1)S(1)} %copy-done.2, bf16[4,768,128]{2,1,0:T(8,128)(2,1)S(1)} %bitcast.3, ...), custom_call_target="tpu_custom_call" | custom-call | flops 2684354560 | bytes 6553600 | tf_op jit(solution)/shard_map/pallas_call | solution.py:129
  82.5 0.6 copy.13
  83.1 16.3 %all-to-all-start = ((f32[16,1,256]{2,1,0:T(1,128)}), f32[16,1,256]{2,1,0:T(1,128)S(1)}, u32[]{:S(2)}, u32[]{:S(2)}) async-start(f32[16,1,256]{2,1,0:T(1,128)} %copy.13), calls=%async_computation | async-start | bytes 32768 | tf_op jit(solution)/shard_map/all_to_all | solution.py:217
  99.4 2.0 %collective-permute-start.12 = (bf16[256,512]{1,0:T(8,128)(2,1)S(1)}, bf16[256,512]{1,0:T(8,128)(2,1)S(1)}, u32[]{:S(2)}, u32[]{:S(2)}) collective-permute-start(bf16[256,512]{1,0:T(8,128)(2,1)S(1)} %get-tuple-element.6), channel_id=1, source_target_pairs={{0,1},{1,0},{2,3},{3,2},{4,5},{5,4},{6,7},{7,6},{8,9},{9,8},{10,11... | collective-permute-start | bytes 786440 | tf_op jit(solution)/shard_map/ppermute | solution.py:58
  101.4 12.5 %all-to-all-done = f32[16,1,256]{2,1,0:T(1,128)S(1)} async-done(((f32[16,1,256]{2,1,0:T(1,128)}), f32[16,1,256]{2,1,0:T(1,128)S(1)}, u32[]{:S(2)}, u32[]{:S(2)}) %all-to-all-start) | async-done | bytes 16416 | tf_op jit(solution)/shard_map/all_to_all | solution.py:217
  114.0 1.1 multiply_convert_fusion
  (46 shorter events, 0.4 us)
Async XLA Ops:
  0.6 20.5 %copy-start.7 = (bf16[256,1024]{1,0:T(8,128)(2,1)S(1)}, bf16[256,1024]{1,0:T(8,128)(2,1)}, u32[]{:S(2)}) copy-start(bf16[256,1024]{1,0:T(8,128)(2,1)} %param.12) | copy-start | bytes 1572868
  0.6 22.9 %copy-start.6 = (bf16[256,1024]{1,0:T(8,128)(2,1)S(1)}, bf16[256,1024]{1,0:T(8,128)(2,1)}, u32[]{:S(2)}) copy-start(bf16[256,1024]{1,0:T(8,128)(2,1)} %param.15) | copy-start | bytes 1572868
  0.7 23.0 %copy-start.9 = (bf16[1024]{0:T(1024)(128)(2,1)S(1)}, bf16[1024]{0:T(1024)(128)(2,1)}, u32[]{:S(2)}) copy-start(bf16[1024]{0:T(1024)(128)(2,1)} %param.14) | copy-start | bytes 6148
  0.7 27.5 %copy-start.5 = (bf16[256,1024]{1,0:T(8,128)(2,1)S(1)}, bf16[256,1024]{1,0:T(8,128)(2,1)}, u32[]{:S(2)}) copy-start(bf16[256,1024]{1,0:T(8,128)(2,1)} %param.11) | copy-start | bytes 1572868
  1.8 11.7 %collective-permute-start = (bf16[256,512]{1,0:T(8,128)(2,1)S(1)}, bf16[256,512]{1,0:T(8,128)(2,1)S(1)}, u32[]{:S(2)}, u32[]{:S(2)}) collective-permute-start(bf16[256,512]{1,0:T(8,128)(2,1)S(1)} %constant_dynamic-slice_fusion.3), channel_id=1, source_target_pairs={{0,1},{1,0},{2,3},{3,2},{64,65},{65,64},{66,67},{67,66},{128,129},... | collective-permute-start | bytes 786440 | tf_op jit(solution)/shard_map/ppermute | solution.py:58
  11.5 16.6 %collective-permute-start.7 = (bf16[256,512]{1,0:T(8,128)(2,1)S(1)}, bf16[256,512]{1,0:T(8,128)(2,1)S(1)}, u32[]{:S(2)}, u32[]{:S(2)}) collective-permute-start(bf16[256,512]{1,0:T(8,128)(2,1)S(1)} %constant_dynamic-slice_fusion.2), channel_id=1, source_target_pairs={{0,1},{1,0},{2,3},{3,2},{4,5},{5,4},{6,7},{7,6},{8,9},{9,8},{10,11... | collective-permute-start | bytes 786440 | tf_op jit(solution)/shard_map/ppermute | solution.py:58
  15.3 8.5 %collective-permute-start.1 = (bf16[512,128]{1,0:T(8,128)(2,1)}, bf16[512,128]{1,0:T(8,128)(2,1)}, u32[]{:S(2)}, u32[]{:S(2)}) collective-permute-start(bf16[512,128]{1,0:T(8,128)(2,1)} %get-tuple-element.21), channel_id=1, source_target_pairs={{0,32},{1,33},{2,34},{3,35},{64,96},{65,97},{66,98},{67,99},{128,1... | collective-permute-start | bytes 393224 | tf_op jit(solution)/shard_map/ppermute | solution.py:58
  17.2 8.4 %collective-permute-start.2 = (bf16[512,128]{1,0:T(8,128)(2,1)}, bf16[512,128]{1,0:T(8,128)(2,1)}, u32[]{:S(2)}, u32[]{:S(2)}) collective-permute-start(bf16[512,128]{1,0:T(8,128)(2,1)} %get-tuple-element.20), channel_id=1, source_target_pairs={{0,16},{1,17},{2,18},{3,19},{64,80},{65,81},{66,82},{67,83},{128,1... | collective-permute-start | bytes 393224 | tf_op jit(solution)/shard_map/ppermute | solution.py:58
  19.2 6.5 %collective-permute-start.3 = (bf16[512,128]{1,0:T(8,128)(2,1)S(1)}, bf16[512,128]{1,0:T(8,128)(2,1)}, u32[]{:S(2)}, u32[]{:S(2)}) collective-permute-start(bf16[512,128]{1,0:T(8,128)(2,1)S(1)} %get-tuple-element.22), channel_id=1, source_target_pairs={{0,48},{1,49},{2,50},{3,51},{64,112},{65,113},{66,114},{67,115},{1... | collective-permute-start | bytes 393224 | tf_op jit(solution)/shard_map/ppermute | solution.py:58
  21.1 11.1 %collective-permute-start.10 = (bf16[256,512]{1,0:T(8,128)(2,1)S(1)}, bf16[256,512]{1,0:T(8,128)(2,1)S(1)}, u32[]{:S(2)}, u32[]{:S(2)}) collective-permute-start(bf16[256,512]{1,0:T(8,128)(2,1)S(1)} %constant_dynamic-slice_fusion.1), channel_id=1, source_target_pairs={{0,1},{1,0},{2,3},{3,2},{4,5},{5,4},{6,7},{7,6},{8,9},{9,8},{10,11... | collective-permute-start | bytes 786440 | tf_op jit(solution)/shard_map/ppermute | solution.py:58
  23.8 8.5 %collective-permute-start.11 = (bf16[256,512]{1,0:T(8,128)(2,1)S(1)}, bf16[256,512]{1,0:T(8,128)(2,1)S(1)}, u32[]{:S(2)}, u32[]{:S(2)}) collective-permute-start(bf16[256,512]{1,0:T(8,128)(2,1)S(1)} %constant_dynamic-slice_fusion), channel_id=1, source_target_pairs={{0,1},{1,0},{2,3},{3,2},{4,5},{5,4},{6,7},{7,6},{8,9},{9,8},{10,11... | collective-permute-start | bytes 786440 | tf_op jit(solution)/shard_map/ppermute | solution.py:58
  26.8 4.1 %collective-permute-start.4 = (bf16[512,128]{1,0:T(8,128)(2,1)S(1)}, bf16[512,128]{1,0:T(8,128)(2,1)S(1)}, u32[]{:S(2)}, u32[]{:S(2)}) collective-permute-start(bf16[512,128]{1,0:T(8,128)(2,1)S(1)} %fusion.2), channel_id=1, source_target_pairs={{0,8},{1,9},{2,10},{3,11},{16,24},{17,25},{18,26},{19,27},{32,40},... | collective-permute-start | bytes 393224 | tf_op jit(solution)/shard_map/ppermute | solution.py:58
  28.3 25.1 %collective-permute-start.8 = (bf16[512,512]{1,0:T(8,128)(2,1)S(1)}, bf16[512,512]{1,0:T(8,128)(2,1)S(1)}, u32[]{:S(2)}, u32[]{:S(2)}) collective-permute-start(bf16[512,512]{1,0:T(8,128)(2,1)S(1)} %pad_maximum_fusion.1.signal), channel_id=1, source_target_pairs={{0,2},{1,3},{2,4},{3,5},{4,6},{5,7},{6,8},{7,9},{8,10},{9,11},{10,... | collective-permute-start | bytes 1572872 | tf_op jit(solution)/shard_map/ppermute | solution.py:58
  30.9 14.1 %collective-permute-start.5 = (bf16[512,128]{1,0:T(8,128)(2,1)S(1)}, bf16[512,128]{1,0:T(8,128)(2,1)S(1)}, u32[]{:S(2)}, u32[]{:S(2)}) collective-permute-start(bf16[512,128]{1,0:T(8,128)(2,1)S(1)} %broadcast_select_fusion.10), channel_id=1, source_target_pairs={{0,4},{1,5},{2,6},{3,7},{8,12},{9,13},{10,14},{11,15},{16,20},{17,... | collective-permute-start | bytes 393224 | tf_op jit(solution)/shard_map/ppermute | solution.py:58
  45.0 11.4 %collective-permute-start.6 = (bf16[512,128]{1,0:T(8,128)(2,1)S(1)}, bf16[512,128]{1,0:T(8,128)(2,1)S(1)}, u32[]{:S(2)}, u32[]{:S(2)}) collective-permute-start(bf16[512,128]{1,0:T(8,128)(2,1)S(1)} %broadcast_select_fusion.11), channel_id=1, source_target_pairs={{0,2},{1,3},{2,0},{3,1},{4,6},{5,7},{6,4},{7,5},{8,10},{9,11},{10,... | collective-permute-start | bytes 393224 | tf_op jit(solution)/shard_map/ppermute | solution.py:58
  53.3 21.5 %copy-start.4 = (bf16[1280,1280]{1,0:T(8,128)(2,1)S(1)}, bf16[1280,1280]{1,0:T(8,128)(2,1)}, u32[]{:S(2)}) copy-start(bf16[1280,1280]{1,0:T(8,128)(2,1)} %constant.86.clone.low) | copy-start | bytes 9830404
  53.4 21.4 %copy-start.3 = (bf16[1280,1280]{1,0:T(8,128)(2,1)S(1)}, bf16[1280,1280]{1,0:T(8,128)(2,1)}, u32[]{:S(2)}) copy-start(bf16[1280,1280]{1,0:T(8,128)(2,1)} %constant.85.clone.high) | copy-start | bytes 9830404
  53.5 21.3 %collective-permute-start.9 = (bf16[256,512]{1,0:T(8,128)(2,1)S(1)}, bf16[256,512]{1,0:T(8,128)(2,1)S(1)}, u32[]{:S(2)}, u32[]{:S(2)}) collective-permute-start(bf16[256,512]{1,0:T(8,128)(2,1)S(1)} %slice.32), channel_id=1, source_target_pairs={{0,2},{1,3},{2,4},{3,5},{4,6},{5,7},{6,8},{7,9},{8,10},{9,11},{10,... | collective-permute-start | bytes 786440 | tf_op jit(solution)/shard_map/ppermute | solution.py:58
  74.9 3.6 %copy-start = (bf16[1280,768]{1,0:T(8,128)(2,1)S(1)}, bf16[1280,768]{1,0:T(8,128)(2,1)}, u32[]{:S(2)}) copy-start(bf16[1280,768]{1,0:T(8,128)(2,1)} %constant.87.clone.high) | copy-start | bytes 5898244
  74.9 3.6 %copy-start.1 = (bf16[1280,768]{1,0:T(8,128)(2,1)S(1)}, bf16[1280,768]{1,0:T(8,128)(2,1)}, u32[]{:S(2)}) copy-start(bf16[1280,768]{1,0:T(8,128)(2,1)} %constant.88.clone.low) | copy-start | bytes 5898244
  74.9 3.6 %copy-start.2 = (bf16[512,1280]{1,0:T(8,128)(2,1)S(1)}, bf16[512,1280]{1,0:T(8,128)(2,1)}, u32[]{:S(2)}) copy-start(bf16[512,1280]{1,0:T(8,128)(2,1)} %constant.89.clone.back) | copy-start | bytes 3932164
  78.5 22.9 %copy-start.8 = (bf16[1024]{0:T(1024)(128)(2,1)S(1)}, bf16[1024]{0:T(1024)(128)(2,1)}, u32[]{:S(2)}) copy-start(bf16[1024]{0:T(1024)(128)(2,1)} %param.16) | copy-start | bytes 6148
  83.1 30.8 %all-to-all-start = ((f32[16,1,256]{2,1,0:T(1,128)}), f32[16,1,256]{2,1,0:T(1,128)S(1)}, u32[]{:S(2)}, u32[]{:S(2)}) async-start(f32[16,1,256]{2,1,0:T(1,128)} %copy.13), calls=%async_computation | async-start | bytes 32768 | tf_op jit(solution)/shard_map/all_to_all | solution.py:217
  99.4 14.5 %collective-permute-start.12 = (bf16[256,512]{1,0:T(8,128)(2,1)S(1)}, bf16[256,512]{1,0:T(8,128)(2,1)S(1)}, u32[]{:S(2)}, u32[]{:S(2)}) collective-permute-start(bf16[256,512]{1,0:T(8,128)(2,1)S(1)} %get-tuple-element.6), channel_id=1, source_target_pairs={{0,1},{1,0},{2,3},{3,2},{4,5},{5,4},{6,7},{7,6},{8,9},{9,8},{10,11... | collective-permute-start | bytes 786440 | tf_op jit(solution)/shard_map/ppermute | solution.py:58

commit v2 on v1

v2 whole, which is shorter than its diff:
```python
import functools
import math

import jax
import jax.numpy as jnp
import ml_dtypes
import numpy as np
from jax import lax
from jax.experimental import pallas as pl
from jax.experimental.pallas import tpu as pltpu
from jax.sharding import PartitionSpec as P

D = 8192
BLOCK = 256
PANELS = 3
HALF = 512
QUARTER = 128
LAGS = PANELS * BLOCK
WINDOW = LAGS + 2 * BLOCK
BINS = WINDOW // 2
TILE = 128
EPS = 1e-05
Y, Z, CORES = 4, 8, 2


@functools.cache
def tables():
    bins = np.arange(BINS)[:, None]
    points = np.arange(WINDOW)[None, :]
    angle = (bins * points % WINDOW) * (2 * math.pi / WINDOW)
    real = np.cos(angle)
    imag = -np.sin(angle)
    imag[0] = (1.0 - 2.0 * (points % 2))[0]
    forward = np.concatenate([real, imag], axis=0)
    scale = np.where(np.arange(BINS) == 0, 1.0, 2.0)[:, None] / WINDOW
    back = np.concatenate([real * scale, imag * scale], axis=0).T[LAGS:]
    return tuple(x.astype(np.float32).astype(ml_dtypes.bfloat16) for x in (forward, back))


def pairs(rule):
    result = []
    for index in range(Y * Z * CORES):
        target = rule(index // (Z * CORES), index // CORES % Z, index % CORES)
        if target is not None:
            y, z, core = target
            result.append((index, y % Y * Z * CORES + z * CORES + core))
    return result


def move(x, rule):
    return lax.ppermute(x, "ctx", pairs(rule))


def dot(a, b):
    return jnp.dot(a, b, preferred_element_type=jnp.float32)


VMEM = pl.BlockSpec(memory_space=pltpu.VMEM)
SMEM = pl.BlockSpec(memory_space=pltpu.SMEM)
HBM = pl.BlockSpec(memory_space=pltpu.HBM)
LIMIT = pltpu.CompilerParams(vmem_limit_bytes=24 * 2**20)


def shaped(*shape, dtype=jnp.bfloat16):
    return jax.ShapeDtypeStruct(shape, dtype)


def columns(which):
    return pl.ds(pl.multiple_of(which * HALF, HALF), HALF)


def others_kernel(core, first, second, out, sems):
    there = columns(1 - core[0])
    copies = [
        pltpu.make_async_copy(x.at[:, there], out.at[i], sems.at[i])
        for i, x in enumerate((first, second))
    ]
    for copy in copies:
        copy.start()
    for copy in copies:
        copy.wait()


def others(core, first, second):
    return pl.pallas_call(
        others_kernel,
        out_shape=shaped(2, BLOCK, HALF),
        in_specs=[SMEM, HBM, HBM],
        out_specs=VMEM,
        scratch_shapes=[pltpu.SemaphoreType.DMA((2,))],
        compiler_params=LIMIT,
    )(core, first, second)


def prepare_kernel(core, taps, signal, other, both, even, odd, *pieces):
    own_rows = pl.ds(pl.multiple_of(core[0] * BLOCK, BLOCK), BLOCK)
    other_rows = pl.ds(pl.multiple_of((1 - core[0]) * BLOCK, BLOCK), BLOCK)
    for q, piece in enumerate(pieces):
        start = pl.multiple_of(core[0] * HALF + q * QUARTER, QUARTER)
        piece[own_rows, :] = taps[:, pl.ds(start, QUARTER)]
        piece[other_rows, :] = other[0, :, q * QUARTER : (q + 1) * QUARTER]

    @pl.when(core[0] == 0)
    def _():
        even[...] = signal[:, :HALF]
        odd[...] = other[1]

    @pl.when(core[0] == 1)
    def _():
        even[...] = other[1]
        odd[...] = signal[:, HALF:]

    both[0] = even[...]
    both[1] = odd[...]


def prepare(core, taps, signal, other):
    return pl.pallas_call(
        prepare_kernel,
        out_shape=(shaped(2, BLOCK, HALF),)
        + (shaped(BLOCK, HALF),) * 2
        + (shaped(2 * BLOCK, QUARTER),) * Y,
        in_specs=[SMEM, VMEM, VMEM, VMEM],
        out_specs=(VMEM,) * (3 + Y),
        compiler_params=LIMIT,
    )(core, taps, signal, other)


def join_kernel(place, held, got, extra, out):
    even = place[0] % 2 == 0

    @pl.when(even)
    def _():
        out[: 2 * BLOCK, :] = held[...]

    @pl.when(jnp.logical_not(even))
    def _():
        out[: 2 * BLOCK, :] = got[...]
        out[2 * BLOCK :, :] = held[:BLOCK, :]

    @pl.when(place[0] == 0)
    def _():
        out[2 * BLOCK :, :] = extra[...]

    @pl.when(jnp.logical_and(even, place[0] > 0))
    def _():
        out[2 * BLOCK :, :] = got[:BLOCK, :]


def join(place, held, got, extra):
    return pl.pallas_call(
        join_kernel,
        out_shape=shaped(LAGS, QUARTER),
        in_specs=[SMEM] + [VMEM] * 3,
        out_specs=VMEM,
        compiler_params=LIMIT,
        cost_estimate=pl.CostEstimate(
            flops=4 * WINDOW * WINDOW * HALF, bytes_accessed=0, transcendentals=0
        ),
    )(place, held, got, extra)


def mix_kernel(
    core,
    place,
    forward,
    back,
    taps,
    far,
    first,
    wrapped,
    before_even,
    before_odd,
    even,
    odd,
    gate,
    residual,
    other_both,
    skip,
    kept,
    sent,
    sums,
    window,
    prod,
):
    filt = jnp.concatenate([taps[q] for q in range(Y)], axis=1)
    window[:BLOCK, :] = jnp.where(place[0] < 2, far[...], first[...])
    window[BLOCK : 2 * BLOCK, :] = jnp.where(place[0] == 0, wrapped[0], before_even[...])
    window[2 * BLOCK : LAGS, :] = jnp.where(place[0] == 0, wrapped[1], before_odd[...])
    window[LAGS : LAGS + BLOCK, :] = even[...]
    window[LAGS + BLOCK :, :] = odd[...]
    for tile in range(BINS // TILE):
        real = slice(tile * TILE, (tile + 1) * TILE)
        imag = slice(BINS + tile * TILE, BINS + (tile + 1) * TILE)
        sr = dot(forward[real, :], window[...])
        si = dot(forward[imag, :], window[...])
        fr = dot(forward[real, :LAGS], filt)
        fi = dot(forward[imag, :LAGS], filt)
        cross = si * fi
        pr = sr * fr - cross
        pi = sr * fi + si * fr
        if tile == 0:
            lowest = lax.broadcasted_iota(jnp.int32, (TILE, HALF), 0) == 0
            pr = jnp.where(lowest, sr * fr, pr)
            pi = jnp.where(lowest, cross, pi)
        prod[real, :] = pr.astype(jnp.bfloat16)
        prod[imag, :] = pi.astype(jnp.bfloat16)
    here = columns(core[0])
    weight = skip[:, here].astype(jnp.float32)

    def update(block, x, g, r, out):
        rows = pl.ds(pl.multiple_of(block * BLOCK, BLOCK), BLOCK)
        conv = dot(back[rows, :], prod[...])
        mixed = g.astype(jnp.float32) * (conv + weight * x.astype(jnp.float32))
        updated = (r.astype(jnp.float32) + mixed).astype(jnp.bfloat16)
        wide = updated.astype(jnp.float32)
        out[...] = updated
        total = jnp.sum(wide * wide, axis=1)[None, :]
        for other in range(8):
            sums[2 * other + block] = total

    lead = core[0] == 0
    theirs = jnp.where(lead, odd[...], even[...])
    ours = jnp.where(lead, even[...], odd[...])
    update(1 - core[0], theirs, other_both[0], other_both[1], sent)
    update(core[0], ours, gate[:, here], residual[:, here], kept)


def mix(core, place, *arrays):
    return pl.pallas_call(
        mix_kernel,
        out_shape=(
            shaped(BLOCK, HALF),
            shaped(BLOCK, HALF),
            shaped(16, 1, BLOCK, dtype=jnp.float32),
        ),
        in_specs=[SMEM, SMEM] + [VMEM] * len(arrays),
        out_specs=(VMEM,) * 3,
        scratch_shapes=[pltpu.VMEM((WINDOW, HALF), jnp.bfloat16)] * 2,
        compiler_params=LIMIT,
        cost_estimate=pl.CostEstimate(
            flops=2 * WINDOW * (WINDOW + LAGS + 2 * BLOCK) * HALF,
            bytes_accessed=2 * WINDOW * LAGS + 4 * WINDOW * HALF,
            transcendentals=0,
        ),
    )(core, place, *arrays)


def finish_kernel(core, kept, received, sums, gain, updated, normed):
    total = sums[0]
    for other in range(1, 16):
        total = total + sums[other]
    scale = lax.rsqrt(total / D + EPS)
    scale = jnp.broadcast_to(scale, (8, BLOCK)).T[:, :1]
    for which, x in ((core[0], kept), (1 - core[0], received)):
        there = columns(which)
        values = x[...].astype(jnp.float32) * scale * gain[:, there].astype(jnp.float32)
        updated[:, there] = x[...]
        normed[:, there] = values.astype(jnp.bfloat16)


def finish(core, kept, received, sums, gain):
    return pl.pallas_call(
        finish_kernel,
        out_shape=(shaped(BLOCK, 2 * HALF),) * 2,
        in_specs=[SMEM] + [VMEM] * 4,
        out_specs=(VMEM, VMEM),
        compiler_params=LIMIT,
    )(core, kept, received, sums, gain)


def local(signal, gate, filter_taps, skip, residual, gain):
    forward, back = tables()
    index = lax.axis_index("ctx")
    y, z, core = index // (Z * CORES), index // CORES % Z, index % CORES
    lead = core == 0

    def flag(x):
        return x.astype(jnp.int32)[None]

    def swap(x):
        return move(x, lambda y, z, c: (y, z, 1 - c))

    other = swap(others(flag(core), filter_taps, signal))
    both, even, odd, *piece = prepare(flag(core), filter_taps, signal, other)
    parts = [
        move(piece[q], lambda y, z, c, q=q: (q, z, c) if y == 0 and z < 2 else None)
        for q in (1, 3, 2)
    ]

    before_odd = move(odd, lambda y, z, c: (y, z + 1, c) if z < Z - 1 else None)
    before_even = move(even, lambda y, z, c: (y, z + 1, c) if z < Z - 1 else None)
    wrapped = move(both, lambda y, z, c: (y + 1, 0, c) if z == Z - 1 else None)
    far = move(odd, lambda y, z, c: (y + 1, z - 6, c) if z >= Z - 2 else None)
    held = jnp.where(y == 0, piece[0], parts[0] + parts[1] + parts[2])
    extra = move(held[:BLOCK], lambda y, z, c: (y, 0, c) if z == 1 else None)
    got = move(held, lambda y, z, c: (y, z + 4, c) if z < 2 else None)
    held = jnp.where(z < 4, held, got)
    got = move(held, lambda y, z, c: (y, z + 2, c) if z % 4 < 2 else None)
    held = jnp.where(z % 4 < 2, held, got)
    first = move(before_odd, lambda y, z, c: (y, z + 1, c) if 0 < z < Z - 1 else None)
    other_both = swap(others(flag(core), gate, residual))
    got = move(held, lambda y, z, c: (y, z + 1, c) if z < Z - 1 else None)
    got, wrapped = lax.optimization_barrier((got, wrapped))
    quarter = join(flag(z), held, got, extra)
    groups = [[(a * Z + b) * CORES + c for a in range(Y)] for b in range(Z) for c in range(CORES)]
    taps = lax.all_gather(quarter, "ctx", axis_index_groups=groups)
    kept, sent, sums = mix(
        flag(core),
        flag(z),
        forward,
        back,
        taps,
        far,
        first,
        wrapped,
        before_even,
        before_odd,
        even,
        odd,
        gate,
        residual,
        other_both,
        skip[None, :],
    )
    size = Y * Z * CORES
    groups = [
        [a * size + b * CORES + c for a in range(8) for c in range(CORES)] for b in range(Y * Z)
    ]
    squares = lax.all_to_all(sums, ("ch", "ctx"), 0, 0, axis_index_groups=groups)
    return finish(flag(core), kept, swap(sent), squares, gain[None, :])


def solution(mesh):
    placed = (P("ctx", "ch"), P("ctx", "ch"), P("ctx", "ch"), P("ch"), P("ctx", "ch"), P("ch"))
    return jax.shard_map(
        local,
        mesh=mesh,
        in_specs=placed,
        out_specs=(P("ctx", "ch"), P("ctx", "ch")),
        check_vma=False,
    )
```

time: 116 us -> 108 us (0.931)
  other arithmetic: 4.83 us -> 0.06 us
  waiting for transfers between devices: 25.6 us -> 21.4 us
  blocking collectives: 18.3 us -> 20.6 us
  Pallas kernels: 7.49 us -> 6.28 us
    ppermute x13 -> x15, waiting for transfers between devices: 13.1 us -> 6.88 us  [move(): return lax.ppermute(x, 'ctx', pairs(rule))]
    all_gather x1, blocking collectives: 18.3 us -> 20.6 us  [local(): taps = lax.all_gather(quarter, 'ctx', axis_index_groups=groups)]
    dynamic_slice x5 -> x0, local copies, waits for them, and re-layouts: 2.18 us -> none  [the longest x4 2.1 us: others(): return lax.dynamic_slice_in_dim(x, (1 - core) * HALF, HALF, axis=1)]
    unnamed x20 -> x16, local copies, waits for them, and re-layouts: 0.06 us -> 2.11 us
    all_to_all x1, waiting for transfers between devices: 12.5 us -> 14.5 us  [local(): lax.all_to_all(sums, ('ch', 'ctx'), 0, 0, axis_index_groups=groups)]
    select_n x6 -> x0, other arithmetic: 1.52 us -> none  [the longest x1 1.04 us: ordered(): jnp.where(lead, other, own)]
    pallas_call x2 -> x6, Pallas kernels: 7.49 us -> 6.28 us  [the longest x1 4.74 us: mix(): pl.pallas_call(mix_kernel, out_shape=(shaped(BLOCK, HALF), shaped(BLOCK,...]
    ppermute x13 -> x15, starting transfers between devices: 38.6 us -> 39.5 us  [move(): return lax.ppermute(x, 'ctx', pairs(rule))]
  transfers between devices with their start and end apart: 14 -> 16, of which waited for: 3 -> 8; matrix products, arithmetic and copies ran while one was open for 4% -> 0% of each run, Pallas kernels for 0% -> 0%
where the time goes in v2:
time: 108 us; the launch traced here: 107 us
  starting transfers between devices  55.8 us (52%)
  waiting for transfers between devices  21.4 us (20%)
  blocking collectives  20.6 us (19%)
  Pallas kernels  6.28 us (6%)
  local copies, waits for them, and re-layouts  2.12 us (2%)
    ppermute x15, starting transfers between devices, move(): return lax.ppermute(x, 'ctx', pairs(rule))  39.5 us
    all_gather x1, blocking collectives, local(): taps = lax.all_gather(quarter, 'ctx', axis_index_groups=groups)  20.6 us
    all_to_all x1, starting transfers between devices, local(): lax.all_to_all(sums, ('ch', 'ctx'), 0, 0, axis_index_groups=groups)  16.3 us
    all_to_all x1, waiting for transfers between devices, local(): lax.all_to_all(sums, ('ch', 'ctx'), 0, 0, axis_index_groups=groups)  14.5 us
    ppermute x15, waiting for transfers between devices, move(): return lax.ppermute(x, 'ctx', pairs(rule))  6.88 us
    pallas_call x1, Pallas kernels, mix(): pl.pallas_call(mix_kernel, out_shape=(shaped(BLOCK, HALF), shaped(BLOCK,...  4.74 us
  transfers between devices with their start and end apart: 16, of which 8 were waited for; matrix products, arithmetic and copies ran while one was open for 0% of the time, Pallas kernels for 0%

profile of v2, /device:TPU:1, one launch (start us, length us, event | category | flops | bytes accessed | tf_op | source)
XLA Modules:
  0.0 107.2 jit_solution(16767606997621979597)
XLA Ops:
  0.7 1.0 copy-done
  1.7 1.0 copy-done.1
  2.7 0.1 shard_map.95
  2.8 8.9 %collective-permute-start = (bf16[2,256,512]{2,1,0:T(8,128)(2,1)S(1)}, bf16[2,256,512]{2,1,0:T(8,128)(2,1)S(1)}, u32[]{:S(2)}, u32[]{:S(2)}) collective-permute-start(bf16[2,256,512]{2,1,0:T(8,128)(2,1)S(1)} %shard_map.95), channel_id=1, source_target_pairs={{0,1},{1,0},{2,3},{3,2},{4,5},{5,4},{6,7},{7,6},{8,9},{9,8},{10,11... | collective-permute-start | bytes 1572872 | tf_op jit(solution)/shard_map/ppermute | solution.py:51
  11.7 1.5 %collective-permute-done.other = bf16[2,256,512]{2,1,0:T(8,128)(2,1)S(1)} collective-permute-done((bf16[2,256,512]{2,1,0:T(8,128)(2,1)S(1)}, bf16[2,256,512]{2,1,0:T(8,128)(2,1)S(1)}, u32[]{:S(2)}, u32[]{:S(2)}) %collective-permute-start) | collective-permute-done | bytes 524320 | tf_op jit(solution)/shard_map/ppermute | solution.py:51
  13.2 0.2 shard_map.96
  13.4 1.3 %collective-permute-start.1 = (bf16[512,128]{1,0:T(8,128)(2,1)S(1)}, bf16[512,128]{1,0:T(8,128)(2,1)S(1)}, u32[]{:S(2)}, u32[]{:S(2)}) collective-permute-start(bf16[512,128]{1,0:T(8,128)(2,1)S(1)} %get-tuple-element.15), channel_id=1, source_target_pairs={{0,16},{1,17},{2,18},{3,19},{64,80},{65,81},{66,82},{67,83},{128,1... | collective-permute-start | bytes 393224 | tf_op jit(solution)/shard_map/ppermute | solution.py:51
  14.7 1.3 %collective-permute-start.2 = (bf16[512,128]{1,0:T(8,128)(2,1)S(1)}, bf16[512,128]{1,0:T(8,128)(2,1)S(1)}, u32[]{:S(2)}, u32[]{:S(2)}) collective-permute-start(bf16[512,128]{1,0:T(8,128)(2,1)S(1)} %get-tuple-element.16), channel_id=1, source_target_pairs={{0,48},{1,49},{2,50},{3,51},{64,112},{65,113},{66,114},{67,115},{1... | collective-permute-start | bytes 393224 | tf_op jit(solution)/shard_map/ppermute | solution.py:51
  16.0 1.3 %collective-permute-start.3 = (bf16[512,128]{1,0:T(8,128)(2,1)S(1)}, bf16[512,128]{1,0:T(8,128)(2,1)S(1)}, u32[]{:S(2)}, u32[]{:S(2)}) collective-permute-start(bf16[512,128]{1,0:T(8,128)(2,1)S(1)} %get-tuple-element.17), channel_id=1, source_target_pairs={{0,32},{1,33},{2,34},{3,35},{64,96},{65,97},{66,98},{67,99},{128,1... | collective-permute-start | bytes 393224 | tf_op jit(solution)/shard_map/ppermute | solution.py:51
  17.4 0.2 collective-permute-done.1
  17.5 1.3 %collective-permute-done.2 = bf16[512,128]{1,0:T(8,128)(2,1)S(1)} collective-permute-done((bf16[512,128]{1,0:T(8,128)(2,1)S(1)}, bf16[512,128]{1,0:T(8,128)(2,1)S(1)}, u32[]{:S(2)}, u32[]{:S(2)}) %collective-permute-start.2) | collective-permute-done | bytes 131104 | tf_op jit(solution)/shard_map/ppermute | solution.py:51
  18.8 1.7 %collective-permute-done.3 = bf16[512,128]{1,0:T(8,128)(2,1)S(1)} collective-permute-done((bf16[512,128]{1,0:T(8,128)(2,1)S(1)}, bf16[512,128]{1,0:T(8,128)(2,1)S(1)}, u32[]{:S(2)}, u32[]{:S(2)}) %collective-permute-start.3) | collective-permute-done | bytes 131104 | tf_op jit(solution)/shard_map/ppermute | solution.py:51
  20.6 1.3 %collective-permute-start.4 = (bf16[512,128]{1,0:T(8,128)(2,1)S(1)}, bf16[512,128]{1,0:T(8,128)(2,1)S(1)}, u32[]{:S(2)}, u32[]{:S(2)}) collective-permute-start(bf16[512,128]{1,0:T(8,128)(2,1)S(1)} %add_select_fusion), channel_id=1, source_target_pairs={{0,8},{1,9},{2,10},{3,11},{16,24},{17,25},{18,26},{19,27},{32,40},... | collective-permute-start | bytes 393224 | tf_op jit(solution)/shard_map/ppermute | solution.py:51
  21.9 1.3 %collective-permute-start.7 = (bf16[2,256,512]{2,1,0:T(8,128)(2,1)S(1)}, bf16[2,256,512]{2,1,0:T(8,128)(2,1)S(1)}, u32[]{:S(2)}, u32[]{:S(2)}) collective-permute-start(bf16[2,256,512]{2,1,0:T(8,128)(2,1)S(1)} %get-tuple-element.18), channel_id=1, source_target_pairs={{14,16},{15,17},{30,32},{31,33},{46,48},{47,49},{62,0},{63,1},{78,... | collective-permute-start | bytes 1572872 | tf_op jit(solution)/shard_map/ppermute | solution.py:51
  23.2 1.2 %collective-permute-done.4 = bf16[512,128]{1,0:T(8,128)(2,1)S(1)} collective-permute-done((bf16[512,128]{1,0:T(8,128)(2,1)S(1)}, bf16[512,128]{1,0:T(8,128)(2,1)S(1)}, u32[]{:S(2)}, u32[]{:S(2)}) %collective-permute-start.4) | collective-permute-done | bytes 131104 | tf_op jit(solution)/shard_map/ppermute | solution.py:51
  24.4 1.3 %collective-permute-start.5 = (bf16[512,128]{1,0:T(8,128)(2,1)S(1)}, bf16[512,128]{1,0:T(8,128)(2,1)S(1)}, u32[]{:S(2)}, u32[]{:S(2)}) collective-permute-start(bf16[512,128]{1,0:T(8,128)(2,1)S(1)} %broadcast_select_fusion), channel_id=1, source_target_pairs={{0,4},{1,5},{2,6},{3,7},{8,12},{9,13},{10,14},{11,15},{16,20},{17,... | collective-permute-start | bytes 393224 | tf_op jit(solution)/shard_map/ppermute | solution.py:51
  25.7 1.3 %collective-permute-start.10 = (bf16[256,512]{1,0:T(8,128)(2,1)S(1)}, bf16[256,512]{1,0:T(8,128)(2,1)S(1)}, u32[]{:S(2)}, u32[]{:S(2)}) collective-permute-start(bf16[256,512]{1,0:T(8,128)(2,1)S(1)} %get-tuple-element.20.odd), channel_id=1, source_target_pairs={{0,2},{1,3},{2,4},{3,5},{4,6},{5,7},{6,8},{7,9},{8,10},{9,11},{10,... | collective-permute-start | bytes 786440 | tf_op jit(solution)/shard_map/ppermute | solution.py:51
  27.0 0.6 collective-permute-done.5
  27.7 5.1 %collective-permute-start.6 = (bf16[512,128]{1,0:T(8,128)(2,1)S(1)}, bf16[512,128]{1,0:T(8,128)(2,1)S(1)}, u32[]{:S(2)}, u32[]{:S(2)}) collective-permute-start(bf16[512,128]{1,0:T(8,128)(2,1)S(1)} %broadcast_select_fusion.1.held), channel_id=1, source_target_pairs={{0,2},{1,3},{2,4},{3,5},{4,6},{5,7},{6,8},{7,9},{8,10},{9,11},{10,... | collective-permute-start | bytes 393224 | tf_op jit(solution)/shard_map/ppermute | solution.py:51
  32.7 1.3 %collective-permute-start.8 = (bf16[256,128]{1,0:T(8,128)(2,1)S(1)}, bf16[256,128]{1,0:T(8,128)(2,1)S(1)}, u32[]{:S(2)}, u32[]{:S(2)}) collective-permute-start(bf16[256,128]{1,0:T(8,128)(2,1)S(1)} %slice.4), channel_id=1, source_target_pairs={{2,0},{3,1},{18,16},{19,17},{34,32},{35,33},{50,48},{51,49},{66,64... | collective-permute-start | bytes 196616 | tf_op jit(solution)/shard_map/ppermute | solution.py:51
  34.1 0.1 shard_map.98
  34.1 5.1 %collective-permute-start.13 = (bf16[2,256,512]{2,1,0:T(8,128)(2,1)S(1)}, bf16[2,256,512]{2,1,0:T(8,128)(2,1)S(1)}, u32[]{:S(2)}, u32[]{:S(2)}) collective-permute-start(bf16[2,256,512]{2,1,0:T(8,128)(2,1)S(1)} %shard_map.98), channel_id=1, source_target_pairs={{0,1},{1,0},{2,3},{3,2},{4,5},{5,4},{6,7},{7,6},{8,9},{9,8},{10,11... | collective-permute-start | bytes 1572872 | tf_op jit(solution)/shard_map/ppermute | solution.py:51
  39.3 1.3 %collective-permute-start.9 = (bf16[256,512]{1,0:T(8,128)(2,1)S(1)}, bf16[256,512]{1,0:T(8,128)(2,1)S(1)}, u32[]{:S(2)}, u32[]{:S(2)}) collective-permute-start(bf16[256,512]{1,0:T(8,128)(2,1)S(1)} %get-tuple-element.20.odd), channel_id=1, source_target_pairs={{12,16},{13,17},{14,18},{15,19},{28,32},{29,33},{30,34},{31,35},{4... | collective-permute-start | bytes 786440 | tf_op jit(solution)/shard_map/ppermute | solution.py:51
  40.6 4.3 %collective-permute-start.12 = (bf16[256,512]{1,0:T(8,128)(2,1)S(1)}, bf16[256,512]{1,0:T(8,128)(2,1)S(1)}, u32[]{:S(2)}, u32[]{:S(2)}) collective-permute-start(bf16[256,512]{1,0:T(8,128)(2,1)S(1)} %get-tuple-element.22.even), channel_id=1, source_target_pairs={{0,2},{1,3},{2,4},{3,5},{4,6},{5,7},{6,8},{7,9},{8,10},{9,11},{10,... | collective-permute-start | bytes 786440 | tf_op jit(solution)/shard_map/ppermute | solution.py:51
  44.9 0.4 collective-permute-done.7.wrapped
  45.3 0.7 collective-permute-start.11
  46.1 20.6 %all-gather = bf16[3072,128]{1,0:T(8,128)(2,1)S(1)} all-gather(bf16[768,128]{1,0:T(8,128)(2,1)S(1)} %shard_map.97), channel_id=2, replica_groups={{0,16,32,48},{1,17,33,49},{2,18,34,50},{3,19,35,51},{4,20,36,52},{5,21,..., dimensions={0}, use_global_device_ids=true | all-gather | bytes 983040 | tf_op jit(solution)/shard_map/all_gather | solution.py:307
  66.7 4.7 %shard_map.99 = (bf16[256,512]{1,0:T(8,128)(2,1)S(1)}, bf16[256,512]{1,0:T(8,128)(2,1)S(1)}, f32[16,1,256]{2,1,0:T(1,128)}) custom-call(s32[1]{0:T(128)} %bitcast.core, s32[1]{0:T(128)} %bitcast.1.place, bf16[1280,1280]{1,0:T(8,128)(2,1)S(1)} %copy-done.4, bf16[512,1280]{1,0:T(8,128)(2,1)S(1)} %copy-done.5, bf16[4,768,128]{2,1,0:T(8,128)(2,1)S(1)} %bitcast.3, ...), custom_call_target="tpu_custom_call" | custom-call | flops 3355443200 | bytes 4587520 | tf_op jit(solution)/shard_map/pallas_call | solution.py:230
  71.4 3.8 %collective-permute-start.14 = (bf16[256,512]{1,0:T(8,128)(2,1)S(1)}, bf16[256,512]{1,0:T(8,128)(2,1)S(1)}, u32[]{:S(2)}, u32[]{:S(2)}) collective-permute-start(bf16[256,512]{1,0:T(8,128)(2,1)S(1)} %get-tuple-element.24), channel_id=1, source_target_pairs={{0,1},{1,0},{2,3},{3,2},{4,5},{5,4},{6,7},{7,6},{8,9},{9,8},{10,11... | collective-permute-start | bytes 786440 | tf_op jit(solution)/shard_map/ppermute | solution.py:51
  75.2 16.3 %all-to-all-start = ((f32[16,1,256]{2,1,0:T(1,128)}), f32[16,1,256]{2,1,0:T(1,128)S(1)}, u32[]{:S(2)}, u32[]{:S(2)}) async-start(f32[16,1,256]{2,1,0:T(1,128)} %get-tuple-element.25), calls=%async_computation | async-start | bytes 32768 | tf_op jit(solution)/shard_map/all_to_all | solution.py:330
  91.5 14.5 %all-to-all-done.sums = f32[16,1,256]{2,1,0:T(1,128)S(1)} async-done(((f32[16,1,256]{2,1,0:T(1,128)}), f32[16,1,256]{2,1,0:T(1,128)S(1)}, u32[]{:S(2)}, u32[]{:S(2)}) %all-to-all-start) | async-done | bytes 16416 | tf_op jit(solution)/shard_map/all_to_all | solution.py:330
  106.0 1.2 %shard_map.100 = (bf16[256,1024]{1,0:T(8,128)(2,1)}, bf16[256,1024]{1,0:T(8,128)(2,1)}) custom-call(s32[1]{0:T(128)} %bitcast.core, bf16[256,512]{1,0:T(8,128)(2,1)S(1)} %get-tuple-element.23.kept, bf16[256,512]{1,0:T(8,128)(2,1)S(1)} %collective-permute-done.14.received, f32[16,1,256]{2,1,0:T(1,128)S(1)} %all-to-all-done.sums, ...), custom_call_target="tpu_custom_call" | custom-call | tf_op jit(solution)/shard_map/pallas_call | solution.py:263
  (29 shorter events, 0.2 us)
Async XLA Ops:
  0.6 38.6 %copy-start.6 = (bf16[1024]{0:T(1024)(128)(2,1)S(1)}, bf16[1024]{0:T(1024)(128)(2,1)}, u32[]{:S(2)}) copy-start(bf16[1024]{0:T(1024)(128)(2,1)} %param.11) | copy-start | bytes 6148
  0.7 1.0 copy-start
  1.7 1.0 copy-start.1
  2.7 31.3 %copy-start.2 = (bf16[256,1024]{1,0:T(8,128)(2,1)S(1)}, bf16[256,1024]{1,0:T(8,128)(2,1)}, u32[]{:S(2)}) copy-start(bf16[256,1024]{1,0:T(8,128)(2,1)} %gate.1) | copy-start | bytes 1572868
  2.7 31.3 %copy-start.3 = (bf16[256,1024]{1,0:T(8,128)(2,1)S(1)}, bf16[256,1024]{1,0:T(8,128)(2,1)}, u32[]{:S(2)}) copy-start(bf16[256,1024]{1,0:T(8,128)(2,1)} %residual.1) | copy-start | bytes 1572868
  2.8 10.4 %collective-permute-start = (bf16[2,256,512]{2,1,0:T(8,128)(2,1)S(1)}, bf16[2,256,512]{2,1,0:T(8,128)(2,1)S(1)}, u32[]{:S(2)}, u32[]{:S(2)}) collective-permute-start(bf16[2,256,512]{2,1,0:T(8,128)(2,1)S(1)} %shard_map.95), channel_id=1, source_target_pairs={{0,1},{1,0},{2,3},{3,2},{4,5},{5,4},{6,7},{7,6},{8,9},{9,8},{10,11... | collective-permute-start | bytes 1572872 | tf_op jit(solution)/shard_map/ppermute | solution.py:51
  13.4 4.1 %collective-permute-start.1 = (bf16[512,128]{1,0:T(8,128)(2,1)S(1)}, bf16[512,128]{1,0:T(8,128)(2,1)S(1)}, u32[]{:S(2)}, u32[]{:S(2)}) collective-permute-start(bf16[512,128]{1,0:T(8,128)(2,1)S(1)} %get-tuple-element.15), channel_id=1, source_target_pairs={{0,16},{1,17},{2,18},{3,19},{64,80},{65,81},{66,82},{67,83},{128,1... | collective-permute-start | bytes 393224 | tf_op jit(solution)/shard_map/ppermute | solution.py:51
  14.7 4.1 %collective-permute-start.2 = (bf16[512,128]{1,0:T(8,128)(2,1)S(1)}, bf16[512,128]{1,0:T(8,128)(2,1)S(1)}, u32[]{:S(2)}, u32[]{:S(2)}) collective-permute-start(bf16[512,128]{1,0:T(8,128)(2,1)S(1)} %get-tuple-element.16), channel_id=1, source_target_pairs={{0,48},{1,49},{2,50},{3,51},{64,112},{65,113},{66,114},{67,115},{1... | collective-permute-start | bytes 393224 | tf_op jit(solution)/shard_map/ppermute | solution.py:51
  16.0 4.5 %collective-permute-start.3 = (bf16[512,128]{1,0:T(8,128)(2,1)S(1)}, bf16[512,128]{1,0:T(8,128)(2,1)S(1)}, u32[]{:S(2)}, u32[]{:S(2)}) collective-permute-start(bf16[512,128]{1,0:T(8,128)(2,1)S(1)} %get-tuple-element.17), channel_id=1, source_target_pairs={{0,32},{1,33},{2,34},{3,35},{64,96},{65,97},{66,98},{67,99},{128,1... | collective-permute-start | bytes 393224 | tf_op jit(solution)/shard_map/ppermute | solution.py:51
  20.6 3.8 %collective-permute-start.4 = (bf16[512,128]{1,0:T(8,128)(2,1)S(1)}, bf16[512,128]{1,0:T(8,128)(2,1)S(1)}, u32[]{:S(2)}, u32[]{:S(2)}) collective-permute-start(bf16[512,128]{1,0:T(8,128)(2,1)S(1)} %add_select_fusion), channel_id=1, source_target_pairs={{0,8},{1,9},{2,10},{3,11},{16,24},{17,25},{18,26},{19,27},{32,40},... | collective-permute-start | bytes 393224 | tf_op jit(solution)/shard_map/ppermute | solution.py:51
  21.9 23.4 %collective-permute-start.7 = (bf16[2,256,512]{2,1,0:T(8,128)(2,1)S(1)}, bf16[2,256,512]{2,1,0:T(8,128)(2,1)S(1)}, u32[]{:S(2)}, u32[]{:S(2)}) collective-permute-start(bf16[2,256,512]{2,1,0:T(8,128)(2,1)S(1)} %get-tuple-element.18), channel_id=1, source_target_pairs={{14,16},{15,17},{30,32},{31,33},{46,48},{47,49},{62,0},{63,1},{78,... | collective-permute-start | bytes 1572872 | tf_op jit(solution)/shard_map/ppermute | solution.py:51
  24.4 3.2 %collective-permute-start.5 = (bf16[512,128]{1,0:T(8,128)(2,1)S(1)}, bf16[512,128]{1,0:T(8,128)(2,1)S(1)}, u32[]{:S(2)}, u32[]{:S(2)}) collective-permute-start(bf16[512,128]{1,0:T(8,128)(2,1)S(1)} %broadcast_select_fusion), channel_id=1, source_target_pairs={{0,4},{1,5},{2,6},{3,7},{8,12},{9,13},{10,14},{11,15},{16,20},{17,... | collective-permute-start | bytes 393224 | tf_op jit(solution)/shard_map/ppermute | solution.py:51
  25.7 13.6 %collective-permute-start.10 = (bf16[256,512]{1,0:T(8,128)(2,1)S(1)}, bf16[256,512]{1,0:T(8,128)(2,1)S(1)}, u32[]{:S(2)}, u32[]{:S(2)}) collective-permute-start(bf16[256,512]{1,0:T(8,128)(2,1)S(1)} %get-tuple-element.20.odd), channel_id=1, source_target_pairs={{0,2},{1,3},{2,4},{3,5},{4,6},{5,7},{6,8},{7,9},{8,10},{9,11},{10,... | collective-permute-start | bytes 786440 | tf_op jit(solution)/shard_map/ppermute | solution.py:51
  27.7 13.0 %collective-permute-start.6 = (bf16[512,128]{1,0:T(8,128)(2,1)S(1)}, bf16[512,128]{1,0:T(8,128)(2,1)S(1)}, u32[]{:S(2)}, u32[]{:S(2)}) collective-permute-start(bf16[512,128]{1,0:T(8,128)(2,1)S(1)} %broadcast_select_fusion.1.held), channel_id=1, source_target_pairs={{0,2},{1,3},{2,4},{3,5},{4,6},{5,7},{6,8},{7,9},{8,10},{9,11},{10,... | collective-permute-start | bytes 393224 | tf_op jit(solution)/shard_map/ppermute | solution.py:51
  32.7 13.2 %collective-permute-start.8 = (bf16[256,128]{1,0:T(8,128)(2,1)S(1)}, bf16[256,128]{1,0:T(8,128)(2,1)S(1)}, u32[]{:S(2)}, u32[]{:S(2)}) collective-permute-start(bf16[256,128]{1,0:T(8,128)(2,1)S(1)} %slice.4), channel_id=1, source_target_pairs={{2,0},{3,1},{18,16},{19,17},{34,32},{35,33},{50,48},{51,49},{66,64... | collective-permute-start | bytes 196616 | tf_op jit(solution)/shard_map/ppermute | solution.py:51
  34.1 32.5 %collective-permute-start.13 = (bf16[2,256,512]{2,1,0:T(8,128)(2,1)S(1)}, bf16[2,256,512]{2,1,0:T(8,128)(2,1)S(1)}, u32[]{:S(2)}, u32[]{:S(2)}) collective-permute-start(bf16[2,256,512]{2,1,0:T(8,128)(2,1)S(1)} %shard_map.98), channel_id=1, source_target_pairs={{0,1},{1,0},{2,3},{3,2},{4,5},{5,4},{6,7},{7,6},{8,9},{9,8},{10,11... | collective-permute-start | bytes 1572872 | tf_op jit(solution)/shard_map/ppermute | solution.py:51
  39.3 27.3 %collective-permute-start.9 = (bf16[256,512]{1,0:T(8,128)(2,1)S(1)}, bf16[256,512]{1,0:T(8,128)(2,1)S(1)}, u32[]{:S(2)}, u32[]{:S(2)}) collective-permute-start(bf16[256,512]{1,0:T(8,128)(2,1)S(1)} %get-tuple-element.20.odd), channel_id=1, source_target_pairs={{12,16},{13,17},{14,18},{15,19},{28,32},{29,33},{30,34},{31,35},{4... | collective-permute-start | bytes 786440 | tf_op jit(solution)/shard_map/ppermute | solution.py:51
  40.6 26.0 %collective-permute-start.12 = (bf16[256,512]{1,0:T(8,128)(2,1)S(1)}, bf16[256,512]{1,0:T(8,128)(2,1)S(1)}, u32[]{:S(2)}, u32[]{:S(2)}) collective-permute-start(bf16[256,512]{1,0:T(8,128)(2,1)S(1)} %get-tuple-element.22.even), channel_id=1, source_target_pairs={{0,2},{1,3},{2,4},{3,5},{4,6},{5,7},{6,8},{7,9},{8,10},{9,11},{10,... | collective-permute-start | bytes 786440 | tf_op jit(solution)/shard_map/ppermute | solution.py:51
  45.3 21.3 %collective-permute-start.11 = (bf16[256,512]{1,0:T(8,128)(2,1)S(1)}, bf16[256,512]{1,0:T(8,128)(2,1)S(1)}, u32[]{:S(2)}, u32[]{:S(2)}) collective-permute-start(bf16[256,512]{1,0:T(8,128)(2,1)S(1)} %collective-permute-done.10.before_odd), channel_id=1, source_target_pairs={{2,4},{3,5},{4,6},{5,7},{6,8},{7,9},{8,10},{9,11},{10,12},{11,13},... | collective-permute-start | bytes 786440 | tf_op jit(solution)/shard_map/ppermute | solution.py:51
  46.0 20.7 %copy-start.4 = (bf16[1280,1280]{1,0:T(8,128)(2,1)S(1)}, bf16[1280,1280]{1,0:T(8,128)(2,1)}, u32[]{:S(2)}) copy-start(bf16[1280,1280]{1,0:T(8,128)(2,1)} %constant.63.clone.forward) | copy-start | bytes 9830404
  46.0 20.6 %copy-start.5 = (bf16[512,1280]{1,0:T(8,128)(2,1)S(1)}, bf16[512,1280]{1,0:T(8,128)(2,1)}, u32[]{:S(2)}) copy-start(bf16[512,1280]{1,0:T(8,128)(2,1)} %constant.64.clone.back) | copy-start | bytes 3932164
  66.7 24.8 %copy-start.7 = (bf16[1024]{0:T(1024)(128)(2,1)S(1)}, bf16[1024]{0:T(1024)(128)(2,1)}, u32[]{:S(2)}) copy-start(bf16[1024]{0:T(1024)(128)(2,1)} %param.13) | copy-start | bytes 6148
  71.4 34.6 %collective-permute-start.14 = (bf16[256,512]{1,0:T(8,128)(2,1)S(1)}, bf16[256,512]{1,0:T(8,128)(2,1)S(1)}, u32[]{:S(2)}, u32[]{:S(2)}) collective-permute-start(bf16[256,512]{1,0:T(8,128)(2,1)S(1)} %get-tuple-element.24), channel_id=1, source_target_pairs={{0,1},{1,0},{2,3},{3,2},{4,5},{5,4},{6,7},{7,6},{8,9},{9,8},{10,11... | collective-permute-start | bytes 786440 | tf_op jit(solution)/shard_map/ppermute | solution.py:51
  75.2 30.8 %all-to-all-start = ((f32[16,1,256]{2,1,0:T(1,128)}), f32[16,1,256]{2,1,0:T(1,128)S(1)}, u32[]{:S(2)}, u32[]{:S(2)}) async-start(f32[16,1,256]{2,1,0:T(1,128)} %get-tuple-element.25), calls=%async_computation | async-start | bytes 32768 | tf_op jit(solution)/shard_map/all_to_all | solution.py:330

commit v3 on v2

--- a/solution.py
+++ b/solution.py
@@ -296,6 +296,7 @@
     extra = move(held[:BLOCK], lambda y, z, c: (y, 0, c) if z == 1 else None)
     got = move(held, lambda y, z, c: (y, z + 4, c) if z < 2 else None)
     held = jnp.where(z < 4, held, got)
+    held, extra = lax.optimization_barrier((held, extra))
     got = move(held, lambda y, z, c: (y, z + 2, c) if z % 4 < 2 else None)
     held = jnp.where(z % 4 < 2, held, got)
     first = move(before_odd, lambda y, z, c: (y, z + 1, c) if 0 < z < Z - 1 else None)

time: 108 us -> 106 us (0.981)
  starting transfers between devices: 55.8 us -> 52.7 us
  blocking collectives: 20.6 us -> 18.8 us
  waiting for transfers between devices: 21.4 us -> 23.2 us
    ppermute x15, waiting for transfers between devices: 6.88 us -> 8.69 us  [move(): return lax.ppermute(x, 'ctx', pairs(rule))]
    all_gather x1, blocking collectives: 20.6 us -> 18.8 us  [local(): taps = lax.all_gather(quarter, 'ctx', axis_index_groups=groups)]
    ppermute x15, starting transfers between devices: 39.5 us -> 38 us  [move(): return lax.ppermute(x, 'ctx', pairs(rule))]
    all_to_all x1, starting transfers between devices: 16.3 us -> 14.7 us  [local(): lax.all_to_all(sums, ('ch', 'ctx'), 0, 0, axis_index_groups=groups)]
  transfers between devices with their start and end apart: 16 -> 16, of which waited for: 8 -> 7; matrix products, arithmetic and copies ran while one was open for 0% -> 0% of each run, Pallas kernels for 0% -> 0%
where the time goes in v3:
time: 106 us; the launch traced here: 104 us
  starting transfers between devices  52.7 us (50%)
  waiting for transfers between devices  23.2 us (22%)
  blocking collectives  18.8 us (18%)
  Pallas kernels  6.29 us (6%)
  local copies, waits for them, and re-layouts  2.12 us (2%)
    ppermute x15, starting transfers between devices, move(): return lax.ppermute(x, 'ctx', pairs(rule))  38 us
    all_gather x1, blocking collectives, local(): taps = lax.all_gather(quarter, 'ctx', axis_index_groups=groups)  18.8 us
    all_to_all x1, starting transfers between devices, local(): lax.all_to_all(sums, ('ch', 'ctx'), 0, 0, axis_index_groups=groups)  14.7 us
    all_to_all x1, waiting for transfers between devices, local(): lax.all_to_all(sums, ('ch', 'ctx'), 0, 0, axis_index_groups=groups)  14.5 us
    ppermute x15, waiting for transfers between devices, move(): return lax.ppermute(x, 'ctx', pairs(rule))  8.69 us
    pallas_call x1, Pallas kernels, mix(): pl.pallas_call(mix_kernel, out_shape=(shaped(BLOCK, HALF), shaped(BLOCK,...  4.75 us
  transfers between devices with their start and end apart: 16, of which 7 were waited for; matrix products, arithmetic and copies ran while one was open for 0% of the time, Pallas kernels for 0%

profile of v3, /device:TPU:1, one launch (start us, length us, event | category | flops | bytes accessed | tf_op | source)
XLA Modules:
  0.0 104.2 jit_solution(9890082369379488693)
XLA Ops:
  0.7 1.0 copy-done
  1.7 1.0 copy-done.1
  2.7 0.1 shard_map.95
  2.8 8.9 %collective-permute-start = (bf16[2,256,512]{2,1,0:T(8,128)(2,1)S(1)}, bf16[2,256,512]{2,1,0:T(8,128)(2,1)S(1)}, u32[]{:S(2)}, u32[]{:S(2)}) collective-permute-start(bf16[2,256,512]{2,1,0:T(8,128)(2,1)S(1)} %shard_map.95), channel_id=1, source_target_pairs={{0,1},{1,0},{2,3},{3,2},{4,5},{5,4},{6,7},{7,6},{8,9},{9,8},{10,11... | collective-permute-start | bytes 1572872 | tf_op jit(solution)/shard_map/ppermute | solution.py:51
  11.7 1.5 %collective-permute-done.other = bf16[2,256,512]{2,1,0:T(8,128)(2,1)S(1)} collective-permute-done((bf16[2,256,512]{2,1,0:T(8,128)(2,1)S(1)}, bf16[2,256,512]{2,1,0:T(8,128)(2,1)S(1)}, u32[]{:S(2)}, u32[]{:S(2)}) %collective-permute-start) | collective-permute-done | bytes 524320 | tf_op jit(solution)/shard_map/ppermute | solution.py:51
  13.2 0.2 shard_map.96
  13.4 1.3 %collective-permute-start.1 = (bf16[512,128]{1,0:T(8,128)(2,1)S(1)}, bf16[512,128]{1,0:T(8,128)(2,1)S(1)}, u32[]{:S(2)}, u32[]{:S(2)}) collective-permute-start(bf16[512,128]{1,0:T(8,128)(2,1)S(1)} %get-tuple-element.17), channel_id=1, source_target_pairs={{0,16},{1,17},{2,18},{3,19},{64,80},{65,81},{66,82},{67,83},{128,1... | collective-permute-start | bytes 393224 | tf_op jit(solution)/shard_map/ppermute | solution.py:51
  14.7 1.3 %collective-permute-start.2 = (bf16[512,128]{1,0:T(8,128)(2,1)S(1)}, bf16[512,128]{1,0:T(8,128)(2,1)S(1)}, u32[]{:S(2)}, u32[]{:S(2)}) collective-permute-start(bf16[512,128]{1,0:T(8,128)(2,1)S(1)} %get-tuple-element.18), channel_id=1, source_target_pairs={{0,48},{1,49},{2,50},{3,51},{64,112},{65,113},{66,114},{67,115},{1... | collective-permute-start | bytes 393224 | tf_op jit(solution)/shard_map/ppermute | solution.py:51
  16.0 1.3 %collective-permute-start.3 = (bf16[512,128]{1,0:T(8,128)(2,1)S(1)}, bf16[512,128]{1,0:T(8,128)(2,1)S(1)}, u32[]{:S(2)}, u32[]{:S(2)}) collective-permute-start(bf16[512,128]{1,0:T(8,128)(2,1)S(1)} %get-tuple-element.19), channel_id=1, source_target_pairs={{0,32},{1,33},{2,34},{3,35},{64,96},{65,97},{66,98},{67,99},{128,1... | collective-permute-start | bytes 393224 | tf_op jit(solution)/shard_map/ppermute | solution.py:51
  17.4 0.2 collective-permute-done.1
  17.5 1.3 %collective-permute-done.2 = bf16[512,128]{1,0:T(8,128)(2,1)S(1)} collective-permute-done((bf16[512,128]{1,0:T(8,128)(2,1)S(1)}, bf16[512,128]{1,0:T(8,128)(2,1)S(1)}, u32[]{:S(2)}, u32[]{:S(2)}) %collective-permute-start.2) | collective-permute-done | bytes 131104 | tf_op jit(solution)/shard_map/ppermute | solution.py:51
  18.8 1.7 %collective-permute-done.3 = bf16[512,128]{1,0:T(8,128)(2,1)S(1)} collective-permute-done((bf16[512,128]{1,0:T(8,128)(2,1)S(1)}, bf16[512,128]{1,0:T(8,128)(2,1)S(1)}, u32[]{:S(2)}, u32[]{:S(2)}) %collective-permute-start.3) | collective-permute-done | bytes 131104 | tf_op jit(solution)/shard_map/ppermute | solution.py:51
  20.6 1.3 %collective-permute-start.4 = (bf16[512,128]{1,0:T(8,128)(2,1)S(1)}, bf16[512,128]{1,0:T(8,128)(2,1)S(1)}, u32[]{:S(2)}, u32[]{:S(2)}) collective-permute-start(bf16[512,128]{1,0:T(8,128)(2,1)S(1)} %add_select_fusion), channel_id=1, source_target_pairs={{0,8},{1,9},{2,10},{3,11},{16,24},{17,25},{18,26},{19,27},{32,40},... | collective-permute-start | bytes 393224 | tf_op jit(solution)/shard_map/ppermute | solution.py:51
  21.9 1.3 %collective-permute-start.8 = (bf16[2,256,512]{2,1,0:T(8,128)(2,1)S(1)}, bf16[2,256,512]{2,1,0:T(8,128)(2,1)S(1)}, u32[]{:S(2)}, u32[]{:S(2)}) collective-permute-start(bf16[2,256,512]{2,1,0:T(8,128)(2,1)S(1)} %get-tuple-element.21), channel_id=1, source_target_pairs={{14,16},{15,17},{30,32},{31,33},{46,48},{47,49},{62,0},{63,1},{78,... | collective-permute-start | bytes 1572872 | tf_op jit(solution)/shard_map/ppermute | solution.py:51
  23.2 1.3 %collective-permute-start.5 = (bf16[256,128]{1,0:T(8,128)(2,1)S(1)}, bf16[256,128]{1,0:T(8,128)(2,1)S(1)}, u32[]{:S(2)}, u32[]{:S(2)}) collective-permute-start(bf16[256,128]{1,0:T(8,128)(2,1)S(1)} %slice.4), channel_id=1, source_target_pairs={{2,0},{3,1},{18,16},{19,17},{34,32},{35,33},{50,48},{51,49},{66,64... | collective-permute-start | bytes 196616 | tf_op jit(solution)/shard_map/ppermute | solution.py:51
  24.6 3.7 %collective-permute-done.5.extra = bf16[256,128]{1,0:T(8,128)(2,1)S(1)} collective-permute-done((bf16[256,128]{1,0:T(8,128)(2,1)S(1)}, bf16[256,128]{1,0:T(8,128)(2,1)S(1)}, u32[]{:S(2)}, u32[]{:S(2)}) %collective-permute-start.5) | collective-permute-done | bytes 65568 | tf_op jit(solution)/shard_map/ppermute | solution.py:51
  28.2 1.3 %collective-permute-start.6 = (bf16[512,128]{1,0:T(8,128)(2,1)S(1)}, bf16[512,128]{1,0:T(8,128)(2,1)S(1)}, u32[]{:S(2)}, u32[]{:S(2)}) collective-permute-start(bf16[512,128]{1,0:T(8,128)(2,1)S(1)} %broadcast_select_fusion), channel_id=1, source_target_pairs={{0,4},{1,5},{2,6},{3,7},{8,12},{9,13},{10,14},{11,15},{16,20},{17,... | collective-permute-start | bytes 393224 | tf_op jit(solution)/shard_map/ppermute | solution.py:51
  29.5 1.6 %collective-permute-start.10 = (bf16[256,512]{1,0:T(8,128)(2,1)S(1)}, bf16[256,512]{1,0:T(8,128)(2,1)S(1)}, u32[]{:S(2)}, u32[]{:S(2)}) collective-permute-start(bf16[256,512]{1,0:T(8,128)(2,1)S(1)} %get-tuple-element.24.odd), channel_id=1, source_target_pairs={{0,2},{1,3},{2,4},{3,5},{4,6},{5,7},{6,8},{7,9},{8,10},{9,11},{10,... | collective-permute-start | bytes 786440 | tf_op jit(solution)/shard_map/ppermute | solution.py:51
  31.2 0.3 collective-permute-done.6
  31.5 1.6 %collective-permute-start.7 = (bf16[512,128]{1,0:T(8,128)(2,1)S(1)}, bf16[512,128]{1,0:T(8,128)(2,1)S(1)}, u32[]{:S(2)}, u32[]{:S(2)}) collective-permute-start(bf16[512,128]{1,0:T(8,128)(2,1)S(1)} %broadcast_select_fusion.1.held), channel_id=1, source_target_pairs={{0,2},{1,3},{2,4},{3,5},{4,6},{5,7},{6,8},{7,9},{8,10},{9,11},{10,... | collective-permute-start | bytes 393224 | tf_op jit(solution)/shard_map/ppermute | solution.py:51
  33.1 0.1 shard_map.98
  33.2 8.2 %collective-permute-start.13 = (bf16[2,256,512]{2,1,0:T(8,128)(2,1)S(1)}, bf16[2,256,512]{2,1,0:T(8,128)(2,1)S(1)}, u32[]{:S(2)}, u32[]{:S(2)}) collective-permute-start(bf16[2,256,512]{2,1,0:T(8,128)(2,1)S(1)} %shard_map.98), channel_id=1, source_target_pairs={{0,1},{1,0},{2,3},{3,2},{4,5},{5,4},{6,7},{7,6},{8,9},{9,8},{10,11... | collective-permute-start | bytes 1572872 | tf_op jit(solution)/shard_map/ppermute | solution.py:51
  41.4 1.3 %collective-permute-start.9 = (bf16[256,512]{1,0:T(8,128)(2,1)S(1)}, bf16[256,512]{1,0:T(8,128)(2,1)S(1)}, u32[]{:S(2)}, u32[]{:S(2)}) collective-permute-start(bf16[256,512]{1,0:T(8,128)(2,1)S(1)} %get-tuple-element.24.odd), channel_id=1, source_target_pairs={{12,16},{13,17},{14,18},{15,19},{28,32},{29,33},{30,34},{31,35},{4... | collective-permute-start | bytes 786440 | tf_op jit(solution)/shard_map/ppermute | solution.py:51
  42.7 3.3 %collective-permute-start.12 = (bf16[256,512]{1,0:T(8,128)(2,1)S(1)}, bf16[256,512]{1,0:T(8,128)(2,1)S(1)}, u32[]{:S(2)}, u32[]{:S(2)}) collective-permute-start(bf16[256,512]{1,0:T(8,128)(2,1)S(1)} %get-tuple-element.26.even), channel_id=1, source_target_pairs={{0,2},{1,3},{2,4},{3,5},{4,6},{5,7},{6,8},{7,9},{8,10},{9,11},{10,... | collective-permute-start | bytes 786440 | tf_op jit(solution)/shard_map/ppermute | solution.py:51
  46.0 0.7 collective-permute-start.11
  46.7 0.0 copy-start.4
  46.8 18.8 %all-gather = bf16[3072,128]{1,0:T(8,128)(2,1)S(1)} all-gather(bf16[768,128]{1,0:T(8,128)(2,1)S(1)} %shard_map.97), channel_id=2, replica_groups={{0,16,32,48},{1,17,33,49},{2,18,34,50},{3,19,35,51},{4,20,36,52},{5,21,..., dimensions={0}, use_global_device_ids=true | all-gather | bytes 983040 | tf_op jit(solution)/shard_map/all_gather | solution.py:308
  65.6 4.7 %shard_map.99 = (bf16[256,512]{1,0:T(8,128)(2,1)S(1)}, bf16[256,512]{1,0:T(8,128)(2,1)S(1)}, f32[16,1,256]{2,1,0:T(1,128)}) custom-call(s32[1]{0:T(128)} %bitcast.core, s32[1]{0:T(128)} %bitcast.1.place, bf16[1280,1280]{1,0:T(8,128)(2,1)S(1)} %copy-done.4, bf16[512,1280]{1,0:T(8,128)(2,1)S(1)} %copy-done.5, bf16[4,768,128]{2,1,0:T(8,128)(2,1)S(1)} %bitcast.3, ...), custom_call_target="tpu_custom_call" | custom-call | flops 3355443200 | bytes 4587520 | tf_op jit(solution)/shard_map/pallas_call | solution.py:230
  70.4 3.4 %collective-permute-start.14 = (bf16[256,512]{1,0:T(8,128)(2,1)S(1)}, bf16[256,512]{1,0:T(8,128)(2,1)S(1)}, u32[]{:S(2)}, u32[]{:S(2)}) collective-permute-start(bf16[256,512]{1,0:T(8,128)(2,1)S(1)} %get-tuple-element.28), channel_id=1, source_target_pairs={{0,1},{1,0},{2,3},{3,2},{4,5},{5,4},{6,7},{7,6},{8,9},{9,8},{10,11... | collective-permute-start | bytes 786440 | tf_op jit(solution)/shard_map/ppermute | solution.py:51
  73.7 14.7 %all-to-all-start = ((f32[16,1,256]{2,1,0:T(1,128)}), f32[16,1,256]{2,1,0:T(1,128)S(1)}, u32[]{:S(2)}, u32[]{:S(2)}) async-start(f32[16,1,256]{2,1,0:T(1,128)} %get-tuple-element.29), calls=%async_computation | async-start | bytes 32768 | tf_op jit(solution)/shard_map/all_to_all | solution.py:331
  88.5 14.5 %all-to-all-done.sums = f32[16,1,256]{2,1,0:T(1,128)S(1)} async-done(((f32[16,1,256]{2,1,0:T(1,128)}), f32[16,1,256]{2,1,0:T(1,128)S(1)}, u32[]{:S(2)}, u32[]{:S(2)}) %all-to-all-start) | async-done | bytes 16416 | tf_op jit(solution)/shard_map/all_to_all | solution.py:331
  103.0 1.2 %shard_map.100 = (bf16[256,1024]{1,0:T(8,128)(2,1)}, bf16[256,1024]{1,0:T(8,128)(2,1)}) custom-call(s32[1]{0:T(128)} %bitcast.core, bf16[256,512]{1,0:T(8,128)(2,1)S(1)} %get-tuple-element.27.kept, bf16[256,512]{1,0:T(8,128)(2,1)S(1)} %collective-permute-done.14.received, f32[16,1,256]{2,1,0:T(1,128)S(1)} %all-to-all-done.sums, ...), custom_call_target="tpu_custom_call" | custom-call | tf_op jit(solution)/shard_map/pallas_call | solution.py:263
  (29 shorter events, 0.2 us)
Async XLA Ops:
  0.6 40.8 %copy-start.6 = (bf16[1024]{0:T(1024)(128)(2,1)S(1)}, bf16[1024]{0:T(1024)(128)(2,1)}, u32[]{:S(2)}) copy-start(bf16[1024]{0:T(1024)(128)(2,1)} %param.11) | copy-start | bytes 6148
  0.7 1.0 %copy-start = (bf16[256,1024]{1,0:T(8,128)(2,1)S(1)}, bf16[256,1024]{1,0:T(8,128)(2,1)}, u32[]{:S(2)}) copy-start(bf16[256,1024]{1,0:T(8,128)(2,1)} %taps.1) | copy-start | bytes 1572868
  1.7 1.0 copy-start.1
  2.7 30.4 %copy-start.2 = (bf16[256,1024]{1,0:T(8,128)(2,1)S(1)}, bf16[256,1024]{1,0:T(8,128)(2,1)}, u32[]{:S(2)}) copy-start(bf16[256,1024]{1,0:T(8,128)(2,1)} %gate.1) | copy-start | bytes 1572868
  2.7 30.4 %copy-start.3 = (bf16[256,1024]{1,0:T(8,128)(2,1)S(1)}, bf16[256,1024]{1,0:T(8,128)(2,1)}, u32[]{:S(2)}) copy-start(bf16[256,1024]{1,0:T(8,128)(2,1)} %residual.1) | copy-start | bytes 1572868
  2.8 10.4 %collective-permute-start = (bf16[2,256,512]{2,1,0:T(8,128)(2,1)S(1)}, bf16[2,256,512]{2,1,0:T(8,128)(2,1)S(1)}, u32[]{:S(2)}, u32[]{:S(2)}) collective-permute-start(bf16[2,256,512]{2,1,0:T(8,128)(2,1)S(1)} %shard_map.95), channel_id=1, source_target_pairs={{0,1},{1,0},{2,3},{3,2},{4,5},{5,4},{6,7},{7,6},{8,9},{9,8},{10,11... | collective-permute-start | bytes 1572872 | tf_op jit(solution)/shard_map/ppermute | solution.py:51
  13.4 4.1 %collective-permute-start.1 = (bf16[512,128]{1,0:T(8,128)(2,1)S(1)}, bf16[512,128]{1,0:T(8,128)(2,1)S(1)}, u32[]{:S(2)}, u32[]{:S(2)}) collective-permute-start(bf16[512,128]{1,0:T(8,128)(2,1)S(1)} %get-tuple-element.17), channel_id=1, source_target_pairs={{0,16},{1,17},{2,18},{3,19},{64,80},{65,81},{66,82},{67,83},{128,1... | collective-permute-start | bytes 393224 | tf_op jit(solution)/shard_map/ppermute | solution.py:51
  14.7 4.1 %collective-permute-start.2 = (bf16[512,128]{1,0:T(8,128)(2,1)S(1)}, bf16[512,128]{1,0:T(8,128)(2,1)S(1)}, u32[]{:S(2)}, u32[]{:S(2)}) collective-permute-start(bf16[512,128]{1,0:T(8,128)(2,1)S(1)} %get-tuple-element.18), channel_id=1, source_target_pairs={{0,48},{1,49},{2,50},{3,51},{64,112},{65,113},{66,114},{67,115},{1... | collective-permute-start | bytes 393224 | tf_op jit(solution)/shard_map/ppermute | solution.py:51
  16.0 4.5 %collective-permute-start.3 = (bf16[512,128]{1,0:T(8,128)(2,1)S(1)}, bf16[512,128]{1,0:T(8,128)(2,1)S(1)}, u32[]{:S(2)}, u32[]{:S(2)}) collective-permute-start(bf16[512,128]{1,0:T(8,128)(2,1)S(1)} %get-tuple-element.19), channel_id=1, source_target_pairs={{0,32},{1,33},{2,34},{3,35},{64,96},{65,97},{66,98},{67,99},{128,1... | collective-permute-start | bytes 393224 | tf_op jit(solution)/shard_map/ppermute | solution.py:51
  20.6 4.0 %collective-permute-start.4 = (bf16[512,128]{1,0:T(8,128)(2,1)S(1)}, bf16[512,128]{1,0:T(8,128)(2,1)S(1)}, u32[]{:S(2)}, u32[]{:S(2)}) collective-permute-start(bf16[512,128]{1,0:T(8,128)(2,1)S(1)} %add_select_fusion), channel_id=1, source_target_pairs={{0,8},{1,9},{2,10},{3,11},{16,24},{17,25},{18,26},{19,27},{32,40},... | collective-permute-start | bytes 393224 | tf_op jit(solution)/shard_map/ppermute | solution.py:51
  21.9 24.8 %collective-permute-start.8 = (bf16[2,256,512]{2,1,0:T(8,128)(2,1)S(1)}, bf16[2,256,512]{2,1,0:T(8,128)(2,1)S(1)}, u32[]{:S(2)}, u32[]{:S(2)}) collective-permute-start(bf16[2,256,512]{2,1,0:T(8,128)(2,1)S(1)} %get-tuple-element.21), channel_id=1, source_target_pairs={{14,16},{15,17},{30,32},{31,33},{46,48},{47,49},{62,0},{63,1},{78,... | collective-permute-start | bytes 1572872 | tf_op jit(solution)/shard_map/ppermute | solution.py:51
  23.2 5.0 %collective-permute-start.5 = (bf16[256,128]{1,0:T(8,128)(2,1)S(1)}, bf16[256,128]{1,0:T(8,128)(2,1)S(1)}, u32[]{:S(2)}, u32[]{:S(2)}) collective-permute-start(bf16[256,128]{1,0:T(8,128)(2,1)S(1)} %slice.4), channel_id=1, source_target_pairs={{2,0},{3,1},{18,16},{19,17},{34,32},{35,33},{50,48},{51,49},{66,64... | collective-permute-start | bytes 196616 | tf_op jit(solution)/shard_map/ppermute | solution.py:51
  28.2 3.2 %collective-permute-start.6 = (bf16[512,128]{1,0:T(8,128)(2,1)S(1)}, bf16[512,128]{1,0:T(8,128)(2,1)S(1)}, u32[]{:S(2)}, u32[]{:S(2)}) collective-permute-start(bf16[512,128]{1,0:T(8,128)(2,1)S(1)} %broadcast_select_fusion), channel_id=1, source_target_pairs={{0,4},{1,5},{2,6},{3,7},{8,12},{9,13},{10,14},{11,15},{16,20},{17,... | collective-permute-start | bytes 393224 | tf_op jit(solution)/shard_map/ppermute | solution.py:51
  29.5 13.2 %collective-permute-start.10 = (bf16[256,512]{1,0:T(8,128)(2,1)S(1)}, bf16[256,512]{1,0:T(8,128)(2,1)S(1)}, u32[]{:S(2)}, u32[]{:S(2)}) collective-permute-start(bf16[256,512]{1,0:T(8,128)(2,1)S(1)} %get-tuple-element.24.odd), channel_id=1, source_target_pairs={{0,2},{1,3},{2,4},{3,5},{4,6},{5,7},{6,8},{7,9},{8,10},{9,11},{10,... | collective-permute-start | bytes 786440 | tf_op jit(solution)/shard_map/ppermute | solution.py:51
  31.5 14.5 %collective-permute-start.7 = (bf16[512,128]{1,0:T(8,128)(2,1)S(1)}, bf16[512,128]{1,0:T(8,128)(2,1)S(1)}, u32[]{:S(2)}, u32[]{:S(2)}) collective-permute-start(bf16[512,128]{1,0:T(8,128)(2,1)S(1)} %broadcast_select_fusion.1.held), channel_id=1, source_target_pairs={{0,2},{1,3},{2,4},{3,5},{4,6},{5,7},{6,8},{7,9},{8,10},{9,11},{10,... | collective-permute-start | bytes 393224 | tf_op jit(solution)/shard_map/ppermute | solution.py:51
  33.2 32.4 %collective-permute-start.13 = (bf16[2,256,512]{2,1,0:T(8,128)(2,1)S(1)}, bf16[2,256,512]{2,1,0:T(8,128)(2,1)S(1)}, u32[]{:S(2)}, u32[]{:S(2)}) collective-permute-start(bf16[2,256,512]{2,1,0:T(8,128)(2,1)S(1)} %shard_map.98), channel_id=1, source_target_pairs={{0,1},{1,0},{2,3},{3,2},{4,5},{5,4},{6,7},{7,6},{8,9},{9,8},{10,11... | collective-permute-start | bytes 1572872 | tf_op jit(solution)/shard_map/ppermute | solution.py:51
  41.4 24.1 %collective-permute-start.9 = (bf16[256,512]{1,0:T(8,128)(2,1)S(1)}, bf16[256,512]{1,0:T(8,128)(2,1)S(1)}, u32[]{:S(2)}, u32[]{:S(2)}) collective-permute-start(bf16[256,512]{1,0:T(8,128)(2,1)S(1)} %get-tuple-element.24.odd), channel_id=1, source_target_pairs={{12,16},{13,17},{14,18},{15,19},{28,32},{29,33},{30,34},{31,35},{4... | collective-permute-start | bytes 786440 | tf_op jit(solution)/shard_map/ppermute | solution.py:51
  42.7 22.8 %collective-permute-start.12 = (bf16[256,512]{1,0:T(8,128)(2,1)S(1)}, bf16[256,512]{1,0:T(8,128)(2,1)S(1)}, u32[]{:S(2)}, u32[]{:S(2)}) collective-permute-start(bf16[256,512]{1,0:T(8,128)(2,1)S(1)} %get-tuple-element.26.even), channel_id=1, source_target_pairs={{0,2},{1,3},{2,4},{3,5},{4,6},{5,7},{6,8},{7,9},{8,10},{9,11},{10,... | collective-permute-start | bytes 786440 | tf_op jit(solution)/shard_map/ppermute | solution.py:51
  46.0 19.6 %collective-permute-start.11 = (bf16[256,512]{1,0:T(8,128)(2,1)S(1)}, bf16[256,512]{1,0:T(8,128)(2,1)S(1)}, u32[]{:S(2)}, u32[]{:S(2)}) collective-permute-start(bf16[256,512]{1,0:T(8,128)(2,1)S(1)} %collective-permute-done.10.before_odd), channel_id=1, source_target_pairs={{2,4},{3,5},{4,6},{5,7},{6,8},{7,9},{8,10},{9,11},{10,12},{11,13},... | collective-permute-start | bytes 786440 | tf_op jit(solution)/shard_map/ppermute | solution.py:51
  46.7 18.9 %copy-start.4 = (bf16[1280,1280]{1,0:T(8,128)(2,1)S(1)}, bf16[1280,1280]{1,0:T(8,128)(2,1)}, u32[]{:S(2)}) copy-start(bf16[1280,1280]{1,0:T(8,128)(2,1)} %constant.63.clone.forward) | copy-start | bytes 9830404
  46.7 18.9 %copy-start.5 = (bf16[512,1280]{1,0:T(8,128)(2,1)S(1)}, bf16[512,1280]{1,0:T(8,128)(2,1)}, u32[]{:S(2)}) copy-start(bf16[512,1280]{1,0:T(8,128)(2,1)} %constant.64.clone.back) | copy-start | bytes 3932164
  65.6 22.9 %copy-start.7 = (bf16[1024]{0:T(1024)(128)(2,1)S(1)}, bf16[1024]{0:T(1024)(128)(2,1)}, u32[]{:S(2)}) copy-start(bf16[1024]{0:T(1024)(128)(2,1)} %param.13) | copy-start | bytes 6148
  70.4 32.6 %collective-permute-start.14 = (bf16[256,512]{1,0:T(8,128)(2,1)S(1)}, bf16[256,512]{1,0:T(8,128)(2,1)S(1)}, u32[]{:S(2)}, u32[]{:S(2)}) collective-permute-start(bf16[256,512]{1,0:T(8,128)(2,1)S(1)} %get-tuple-element.28), channel_id=1, source_target_pairs={{0,1},{1,0},{2,3},{3,2},{4,5},{5,4},{6,7},{7,6},{8,9},{9,8},{10,11... | collective-permute-start | bytes 786440 | tf_op jit(solution)/shard_map/ppermute | solution.py:51
  73.7 29.2 %all-to-all-start = ((f32[16,1,256]{2,1,0:T(1,128)}), f32[16,1,256]{2,1,0:T(1,128)S(1)}, u32[]{:S(2)}, u32[]{:S(2)}) async-start(f32[16,1,256]{2,1,0:T(1,128)} %get-tuple-element.29), calls=%async_computation | async-start | bytes 32768 | tf_op jit(solution)/shard_map/all_to_all | solution.py:331

commit v4 on v3

--- a/solution.py
+++ b/solution.py
@@ -246,29 +246,6 @@
     )(core, place, *arrays)
 
 
-def finish_kernel(core, kept, received, sums, gain, updated, normed):
-    total = sums[0]
-    for other in range(1, 16):
-        total = total + sums[other]
-    scale = lax.rsqrt(total / D + EPS)
-    scale = jnp.broadcast_to(scale, (8, BLOCK)).T[:, :1]
-    for which, x in ((core[0], kept), (1 - core[0], received)):
-        there = columns(which)
-        values = x[...].astype(jnp.float32) * scale * gain[:, there].astype(jnp.float32)
-        updated[:, there] = x[...]
-        normed[:, there] = values.astype(jnp.bfloat16)
-
-
-def finish(core, kept, received, sums, gain):
-    return pl.pallas_call(
-        finish_kernel,
-        out_shape=(shaped(BLOCK, 2 * HALF),) * 2,
-        in_specs=[SMEM] + [VMEM] * 4,
-        out_specs=(VMEM, VMEM),
-        compiler_params=LIMIT,
-    )(core, kept, received, sums, gain)
-
-
 def local(signal, gate, filter_taps, skip, residual, gain):
     forward, back = tables()
     index = lax.axis_index("ctx")
@@ -329,7 +306,14 @@
         [a * size + b * CORES + c for a in range(8) for c in range(CORES)] for b in range(Y * Z)
     ]
     squares = lax.all_to_all(sums, ("ch", "ctx"), 0, 0, axis_index_groups=groups)
-    return finish(flag(core), kept, swap(sent), squares, gain[None, :])
+    received = swap(sent)
+    lead = core == 0
+    new_residual = jnp.concatenate(
+        [jnp.where(lead, kept, received), jnp.where(lead, received, kept)], axis=1
+    )
+    scale = lax.rsqrt(jnp.sum(squares[:, 0], axis=0) / D + EPS)[:, None]
+    normed = new_residual.astype(jnp.float32) * scale * gain.astype(jnp.float32)[None, :]
+    return (new_residual, normed.astype(jnp.bfloat16))
 
 
 def solution(mesh):

time: 106 us -> 104 us (0.981)
  waiting for transfers between devices: 23.2 us -> 21.1 us
  other arithmetic: 0.06 us -> 1.29 us
  Pallas kernels: 6.29 us -> 5.08 us
    all_to_all x1, waiting for transfers between devices: 14.5 us -> 12.5 us  [local(): lax.all_to_all(sums, ('ch', 'ctx'), 0, 0, axis_index_groups=groups)]
    ppermute x15, starting transfers between devices: 38 us -> 36.6 us  [move(): return lax.ppermute(x, 'ctx', pairs(rule))]
    all_to_all x1, starting transfers between devices: 14.7 us -> 16.1 us  [local(): lax.all_to_all(sums, ('ch', 'ctx'), 0, 0, axis_index_groups=groups)]
    pallas_call x1 -> x0, Pallas kernels: 1.21 us -> none  [finish(): pl.pallas_call(finish_kernel, out_shape=(shaped(BLOCK, 2 * HALF),) * 2, i...]
    convert_element_type x0 -> x2, other arithmetic: none -> 1.15 us  [the longest x1 1.15 us: local(): return (new_residual, normed.astype(jnp.bfloat16))]
where the time goes in v4:
time: 104 us; the launch traced here: 102 us
  starting transfers between devices  52.7 us (51%)
  waiting for transfers between devices  21.1 us (20%)
  blocking collectives  18.8 us (18%)
  Pallas kernels  5.08 us (5%)
  local copies, waits for them, and re-layouts  2.12 us (2%)
  other arithmetic  1.29 us (1%)
  between operations  1.05 us (1%)
    ppermute x15, starting transfers between devices, move(): return lax.ppermute(x, 'ctx', pairs(rule))  36.6 us
    all_gather x1, blocking collectives, local(): taps = lax.all_gather(quarter, 'ctx', axis_index_groups=groups)  18.8 us
    all_to_all x1, starting transfers between devices, local(): lax.all_to_all(sums, ('ch', 'ctx'), 0, 0, axis_index_groups=groups)  16.1 us
    all_to_all x1, waiting for transfers between devices, local(): lax.all_to_all(sums, ('ch', 'ctx'), 0, 0, axis_index_groups=groups)  12.5 us
    ppermute x15, waiting for transfers between devices, move(): return lax.ppermute(x, 'ctx', pairs(rule))  8.69 us
    pallas_call x1, Pallas kernels, mix(): pl.pallas_call(mix_kernel, out_shape=(shaped(BLOCK, HALF), shaped(BLOCK,...  4.75 us
    unnamed x16, local copies, waits for them, and re-layouts  2.11 us
  transfers between devices with their start and end apart: 16, of which 7 were waited for; matrix products, arithmetic and copies ran while one was open for 0% of the time, Pallas kernels for 0%

profile of v4, /device:TPU:1, one launch (start us, length us, event | category | flops | bytes accessed | tf_op | source)
XLA Modules:
  0.0 102.2 jit_solution(14000448272063866416)
XLA Ops:
  0.7 1.0 %copy-done = bf16[256,1024]{1,0:T(8,128)(2,1)S(1)} copy-done((bf16[256,1024]{1,0:T(8,128)(2,1)S(1)}, bf16[256,1024]{1,0:T(8,128)(2,1)}, u32[]{:S(2)}) %copy-start) | copy-done | bytes 524312
  1.7 1.0 %copy-done.1 = bf16[256,1024]{1,0:T(8,128)(2,1)S(1)} copy-done((bf16[256,1024]{1,0:T(8,128)(2,1)S(1)}, bf16[256,1024]{1,0:T(8,128)(2,1)}, u32[]{:S(2)}) %copy-start.1) | copy-done | bytes 524312
  2.7 0.1 shard_map.95
  2.8 8.9 %collective-permute-start = (bf16[2,256,512]{2,1,0:T(8,128)(2,1)S(1)}, bf16[2,256,512]{2,1,0:T(8,128)(2,1)S(1)}, u32[]{:S(2)}, u32[]{:S(2)}) collective-permute-start(bf16[2,256,512]{2,1,0:T(8,128)(2,1)S(1)} %shard_map.95), channel_id=1, source_target_pairs={{0,1},{1,0},{2,3},{3,2},{4,5},{5,4},{6,7},{7,6},{8,9},{9,8},{10,11... | collective-permute-start | bytes 1572872 | tf_op jit(solution)/shard_map/ppermute | solution.py:51
  11.7 1.5 %collective-permute-done.other = bf16[2,256,512]{2,1,0:T(8,128)(2,1)S(1)} collective-permute-done((bf16[2,256,512]{2,1,0:T(8,128)(2,1)S(1)}, bf16[2,256,512]{2,1,0:T(8,128)(2,1)S(1)}, u32[]{:S(2)}, u32[]{:S(2)}) %collective-permute-start) | collective-permute-done | bytes 524320 | tf_op jit(solution)/shard_map/ppermute | solution.py:51
  13.2 0.2 shard_map.96
  13.4 1.3 %collective-permute-start.1 = (bf16[512,128]{1,0:T(8,128)(2,1)S(1)}, bf16[512,128]{1,0:T(8,128)(2,1)S(1)}, u32[]{:S(2)}, u32[]{:S(2)}) collective-permute-start(bf16[512,128]{1,0:T(8,128)(2,1)S(1)} %get-tuple-element.17), channel_id=1, source_target_pairs={{0,16},{1,17},{2,18},{3,19},{64,80},{65,81},{66,82},{67,83},{128,1... | collective-permute-start | bytes 393224 | tf_op jit(solution)/shard_map/ppermute | solution.py:51
  14.7 1.3 %collective-permute-start.2 = (bf16[512,128]{1,0:T(8,128)(2,1)S(1)}, bf16[512,128]{1,0:T(8,128)(2,1)S(1)}, u32[]{:S(2)}, u32[]{:S(2)}) collective-permute-start(bf16[512,128]{1,0:T(8,128)(2,1)S(1)} %get-tuple-element.18), channel_id=1, source_target_pairs={{0,48},{1,49},{2,50},{3,51},{64,112},{65,113},{66,114},{67,115},{1... | collective-permute-start | bytes 393224 | tf_op jit(solution)/shard_map/ppermute | solution.py:51
  16.0 1.3 %collective-permute-start.3 = (bf16[512,128]{1,0:T(8,128)(2,1)S(1)}, bf16[512,128]{1,0:T(8,128)(2,1)S(1)}, u32[]{:S(2)}, u32[]{:S(2)}) collective-permute-start(bf16[512,128]{1,0:T(8,128)(2,1)S(1)} %get-tuple-element.19), channel_id=1, source_target_pairs={{0,32},{1,33},{2,34},{3,35},{64,96},{65,97},{66,98},{67,99},{128,1... | collective-permute-start | bytes 393224 | tf_op jit(solution)/shard_map/ppermute | solution.py:51
  17.4 0.2 collective-permute-done.1
  17.5 1.3 %collective-permute-done.2 = bf16[512,128]{1,0:T(8,128)(2,1)S(1)} collective-permute-done((bf16[512,128]{1,0:T(8,128)(2,1)S(1)}, bf16[512,128]{1,0:T(8,128)(2,1)S(1)}, u32[]{:S(2)}, u32[]{:S(2)}) %collective-permute-start.2) | collective-permute-done | bytes 131104 | tf_op jit(solution)/shard_map/ppermute | solution.py:51
  18.8 1.7 %collective-permute-done.3 = bf16[512,128]{1,0:T(8,128)(2,1)S(1)} collective-permute-done((bf16[512,128]{1,0:T(8,128)(2,1)S(1)}, bf16[512,128]{1,0:T(8,128)(2,1)S(1)}, u32[]{:S(2)}, u32[]{:S(2)}) %collective-permute-start.3) | collective-permute-done | bytes 131104 | tf_op jit(solution)/shard_map/ppermute | solution.py:51
  20.6 1.3 %collective-permute-start.4 = (bf16[512,128]{1,0:T(8,128)(2,1)S(1)}, bf16[512,128]{1,0:T(8,128)(2,1)S(1)}, u32[]{:S(2)}, u32[]{:S(2)}) collective-permute-start(bf16[512,128]{1,0:T(8,128)(2,1)S(1)} %add_select_fusion), channel_id=1, source_target_pairs={{0,8},{1,9},{2,10},{3,11},{16,24},{17,25},{18,26},{19,27},{32,40},... | collective-permute-start | bytes 393224 | tf_op jit(solution)/shard_map/ppermute | solution.py:51
  21.9 1.3 %collective-permute-start.8 = (bf16[2,256,512]{2,1,0:T(8,128)(2,1)S(1)}, bf16[2,256,512]{2,1,0:T(8,128)(2,1)S(1)}, u32[]{:S(2)}, u32[]{:S(2)}) collective-permute-start(bf16[2,256,512]{2,1,0:T(8,128)(2,1)S(1)} %get-tuple-element.21), channel_id=1, source_target_pairs={{14,16},{15,17},{30,32},{31,33},{46,48},{47,49},{62,0},{63,1},{78,... | collective-permute-start | bytes 1572872 | tf_op jit(solution)/shard_map/ppermute | solution.py:51
  23.2 1.3 %collective-permute-start.5 = (bf16[256,128]{1,0:T(8,128)(2,1)S(1)}, bf16[256,128]{1,0:T(8,128)(2,1)S(1)}, u32[]{:S(2)}, u32[]{:S(2)}) collective-permute-start(bf16[256,128]{1,0:T(8,128)(2,1)S(1)} %slice.4), channel_id=1, source_target_pairs={{2,0},{3,1},{18,16},{19,17},{34,32},{35,33},{50,48},{51,49},{66,64... | collective-permute-start | bytes 196616 | tf_op jit(solution)/shard_map/ppermute | solution.py:51
  24.6 3.7 %collective-permute-done.5.extra = bf16[256,128]{1,0:T(8,128)(2,1)S(1)} collective-permute-done((bf16[256,128]{1,0:T(8,128)(2,1)S(1)}, bf16[256,128]{1,0:T(8,128)(2,1)S(1)}, u32[]{:S(2)}, u32[]{:S(2)}) %collective-permute-start.5) | collective-permute-done | bytes 65568 | tf_op jit(solution)/shard_map/ppermute | solution.py:51
  28.2 1.3 %collective-permute-start.6 = (bf16[512,128]{1,0:T(8,128)(2,1)S(1)}, bf16[512,128]{1,0:T(8,128)(2,1)S(1)}, u32[]{:S(2)}, u32[]{:S(2)}) collective-permute-start(bf16[512,128]{1,0:T(8,128)(2,1)S(1)} %broadcast_select_fusion.2), channel_id=1, source_target_pairs={{0,4},{1,5},{2,6},{3,7},{8,12},{9,13},{10,14},{11,15},{16,20},{17,... | collective-permute-start | bytes 393224 | tf_op jit(solution)/shard_map/ppermute | solution.py:51
  29.5 1.6 %collective-permute-start.10 = (bf16[256,512]{1,0:T(8,128)(2,1)S(1)}, bf16[256,512]{1,0:T(8,128)(2,1)S(1)}, u32[]{:S(2)}, u32[]{:S(2)}) collective-permute-start(bf16[256,512]{1,0:T(8,128)(2,1)S(1)} %get-tuple-element.24.odd), channel_id=1, source_target_pairs={{0,2},{1,3},{2,4},{3,5},{4,6},{5,7},{6,8},{7,9},{8,10},{9,11},{10,... | collective-permute-start | bytes 786440 | tf_op jit(solution)/shard_map/ppermute | solution.py:51
  31.2 0.3 collective-permute-done.6
  31.5 1.6 %collective-permute-start.7 = (bf16[512,128]{1,0:T(8,128)(2,1)S(1)}, bf16[512,128]{1,0:T(8,128)(2,1)S(1)}, u32[]{:S(2)}, u32[]{:S(2)}) collective-permute-start(bf16[512,128]{1,0:T(8,128)(2,1)S(1)} %broadcast_select_fusion.3.held), channel_id=1, source_target_pairs={{0,2},{1,3},{2,4},{3,5},{4,6},{5,7},{6,8},{7,9},{8,10},{9,11},{10,... | collective-permute-start | bytes 393224 | tf_op jit(solution)/shard_map/ppermute | solution.py:51
  33.1 0.1 shard_map.98
  33.2 8.2 %collective-permute-start.13 = (bf16[2,256,512]{2,1,0:T(8,128)(2,1)S(1)}, bf16[2,256,512]{2,1,0:T(8,128)(2,1)S(1)}, u32[]{:S(2)}, u32[]{:S(2)}) collective-permute-start(bf16[2,256,512]{2,1,0:T(8,128)(2,1)S(1)} %shard_map.98), channel_id=1, source_target_pairs={{0,1},{1,0},{2,3},{3,2},{4,5},{5,4},{6,7},{7,6},{8,9},{9,8},{10,11... | collective-permute-start | bytes 1572872 | tf_op jit(solution)/shard_map/ppermute | solution.py:51
  41.4 1.3 %collective-permute-start.9 = (bf16[256,512]{1,0:T(8,128)(2,1)S(1)}, bf16[256,512]{1,0:T(8,128)(2,1)S(1)}, u32[]{:S(2)}, u32[]{:S(2)}) collective-permute-start(bf16[256,512]{1,0:T(8,128)(2,1)S(1)} %get-tuple-element.24.odd), channel_id=1, source_target_pairs={{12,16},{13,17},{14,18},{15,19},{28,32},{29,33},{30,34},{31,35},{4... | collective-permute-start | bytes 786440 | tf_op jit(solution)/shard_map/ppermute | solution.py:51
  42.7 3.3 %collective-permute-start.12 = (bf16[256,512]{1,0:T(8,128)(2,1)S(1)}, bf16[256,512]{1,0:T(8,128)(2,1)S(1)}, u32[]{:S(2)}, u32[]{:S(2)}) collective-permute-start(bf16[256,512]{1,0:T(8,128)(2,1)S(1)} %get-tuple-element.26.even), channel_id=1, source_target_pairs={{0,2},{1,3},{2,4},{3,5},{4,6},{5,7},{6,8},{7,9},{8,10},{9,11},{10,... | collective-permute-start | bytes 786440 | tf_op jit(solution)/shard_map/ppermute | solution.py:51
  46.0 0.7 collective-permute-start.11
  46.7 0.0 copy-start.4
  46.8 18.8 %all-gather = bf16[3072,128]{1,0:T(8,128)(2,1)S(1)} all-gather(bf16[768,128]{1,0:T(8,128)(2,1)S(1)} %shard_map.97), channel_id=2, replica_groups={{0,16,32,48},{1,17,33,49},{2,18,34,50},{3,19,35,51},{4,20,36,52},{5,21,..., dimensions={0}, use_global_device_ids=true | all-gather | bytes 983040 | tf_op jit(solution)/shard_map/all_gather | solution.py:285
  65.6 4.7 %shard_map.99 = (bf16[256,512]{1,0:T(8,128)(2,1)S(1)}, bf16[256,512]{1,0:T(8,128)(2,1)S(1)}, f32[16,1,256]{2,1,0:T(1,128)}) custom-call(s32[1]{0:T(128)} %bitcast.core, s32[1]{0:T(128)} %bitcast.1.place, bf16[1280,1280]{1,0:T(8,128)(2,1)S(1)} %copy-done.4, bf16[512,1280]{1,0:T(8,128)(2,1)S(1)} %copy-done.5, bf16[4,768,128]{2,1,0:T(8,128)(2,1)S(1)} %bitcast.3, ...), custom_call_target="tpu_custom_call" | custom-call | flops 3355443200 | bytes 4587520 | tf_op jit(solution)/shard_map/pallas_call | solution.py:230
  70.4 16.1 %all-to-all-start = ((f32[16,1,256]{2,1,0:T(1,128)}), f32[16,1,256]{2,1,0:T(1,128)S(1)}, u32[]{:S(2)}, u32[]{:S(2)}) async-start(f32[16,1,256]{2,1,0:T(1,128)} %get-tuple-element.29), calls=%async_computation | async-start | bytes 32768 | tf_op jit(solution)/shard_map/all_to_all | solution.py:308
  86.4 2.0 %collective-permute-start.14 = (bf16[256,512]{1,0:T(8,128)(2,1)S(1)}, bf16[256,512]{1,0:T(8,128)(2,1)S(1)}, u32[]{:S(2)}, u32[]{:S(2)}) collective-permute-start(bf16[256,512]{1,0:T(8,128)(2,1)S(1)} %get-tuple-element.28), channel_id=1, source_target_pairs={{0,1},{1,0},{2,3},{3,2},{4,5},{5,4},{6,7},{7,6},{8,9},{9,8},{10,11... | collective-permute-start | bytes 786440 | tf_op jit(solution)/shard_map/ppermute | solution.py:51
  88.5 12.5 %all-to-all-done = f32[16,1,256]{2,1,0:T(1,128)S(1)} async-done(((f32[16,1,256]{2,1,0:T(1,128)}), f32[16,1,256]{2,1,0:T(1,128)S(1)}, u32[]{:S(2)}, u32[]{:S(2)}) %all-to-all-start) | async-done | bytes 16416 | tf_op jit(solution)/shard_map/all_to_all | solution.py:308
  101.0 1.1 %multiply_convert_fusion = (bf16[256,1024]{1,0:T(8,128)(2,1)}, bf16[256,1024]{1,0:T(8,128)(2,1)}) fusion(f32[1024]{0:T(1024)S(1)} %convert_element_type.10, f32[256]{0:T(256)S(1)} %add_rsqrt_fusion, bf16[256,512]{1,0:T(8,128)(2,1)S(1)} %get-tuple-element.33, bf16[256,512]{1,0:T(8,128)(2,1)S(1)} %get-tuple-element.32), kind=kLoop, calls=%fused_computation | loop fusion | flops 2097152 | bytes 1577984 | tf_op jit(solution)/shard_map/convert_element_type | solution.py:316
  (32 shorter events, 0.3 us)
Async XLA Ops:
  0.6 40.8 %copy-start.6 = (bf16[1024]{0:T(1024)(128)(2,1)S(1)}, bf16[1024]{0:T(1024)(128)(2,1)}, u32[]{:S(2)}) copy-start(bf16[1024]{0:T(1024)(128)(2,1)} %param.11) | copy-start | bytes 6148
  0.7 1.0 %copy-start = (bf16[256,1024]{1,0:T(8,128)(2,1)S(1)}, bf16[256,1024]{1,0:T(8,128)(2,1)}, u32[]{:S(2)}) copy-start(bf16[256,1024]{1,0:T(8,128)(2,1)} %taps.1) | copy-start | bytes 1572868
  1.7 1.0 %copy-start.1 = (bf16[256,1024]{1,0:T(8,128)(2,1)S(1)}, bf16[256,1024]{1,0:T(8,128)(2,1)}, u32[]{:S(2)}) copy-start(bf16[256,1024]{1,0:T(8,128)(2,1)} %signal.1) | copy-start | bytes 1572868
  2.7 30.4 %copy-start.2 = (bf16[256,1024]{1,0:T(8,128)(2,1)S(1)}, bf16[256,1024]{1,0:T(8,128)(2,1)}, u32[]{:S(2)}) copy-start(bf16[256,1024]{1,0:T(8,128)(2,1)} %gate.1) | copy-start | bytes 1572868
  2.7 30.4 %copy-start.3 = (bf16[256,1024]{1,0:T(8,128)(2,1)S(1)}, bf16[256,1024]{1,0:T(8,128)(2,1)}, u32[]{:S(2)}) copy-start(bf16[256,1024]{1,0:T(8,128)(2,1)} %residual.1) | copy-start | bytes 1572868
  2.8 10.4 %collective-permute-start = (bf16[2,256,512]{2,1,0:T(8,128)(2,1)S(1)}, bf16[2,256,512]{2,1,0:T(8,128)(2,1)S(1)}, u32[]{:S(2)}, u32[]{:S(2)}) collective-permute-start(bf16[2,256,512]{2,1,0:T(8,128)(2,1)S(1)} %shard_map.95), channel_id=1, source_target_pairs={{0,1},{1,0},{2,3},{3,2},{4,5},{5,4},{6,7},{7,6},{8,9},{9,8},{10,11... | collective-permute-start | bytes 1572872 | tf_op jit(solution)/shard_map/ppermute | solution.py:51
  13.4 4.1 %collective-permute-start.1 = (bf16[512,128]{1,0:T(8,128)(2,1)S(1)}, bf16[512,128]{1,0:T(8,128)(2,1)S(1)}, u32[]{:S(2)}, u32[]{:S(2)}) collective-permute-start(bf16[512,128]{1,0:T(8,128)(2,1)S(1)} %get-tuple-element.17), channel_id=1, source_target_pairs={{0,16},{1,17},{2,18},{3,19},{64,80},{65,81},{66,82},{67,83},{128,1... | collective-permute-start | bytes 393224 | tf_op jit(solution)/shard_map/ppermute | solution.py:51
  14.7 4.1 %collective-permute-start.2 = (bf16[512,128]{1,0:T(8,128)(2,1)S(1)}, bf16[512,128]{1,0:T(8,128)(2,1)S(1)}, u32[]{:S(2)}, u32[]{:S(2)}) collective-permute-start(bf16[512,128]{1,0:T(8,128)(2,1)S(1)} %get-tuple-element.18), channel_id=1, source_target_pairs={{0,48},{1,49},{2,50},{3,51},{64,112},{65,113},{66,114},{67,115},{1... | collective-permute-start | bytes 393224 | tf_op jit(solution)/shard_map/ppermute | solution.py:51
  16.0 4.5 %collective-permute-start.3 = (bf16[512,128]{1,0:T(8,128)(2,1)S(1)}, bf16[512,128]{1,0:T(8,128)(2,1)S(1)}, u32[]{:S(2)}, u32[]{:S(2)}) collective-permute-start(bf16[512,128]{1,0:T(8,128)(2,1)S(1)} %get-tuple-element.19), channel_id=1, source_target_pairs={{0,32},{1,33},{2,34},{3,35},{64,96},{65,97},{66,98},{67,99},{128,1... | collective-permute-start | bytes 393224 | tf_op jit(solution)/shard_map/ppermute | solution.py:51
  20.6 4.0 %collective-permute-start.4 = (bf16[512,128]{1,0:T(8,128)(2,1)S(1)}, bf16[512,128]{1,0:T(8,128)(2,1)S(1)}, u32[]{:S(2)}, u32[]{:S(2)}) collective-permute-start(bf16[512,128]{1,0:T(8,128)(2,1)S(1)} %add_select_fusion), channel_id=1, source_target_pairs={{0,8},{1,9},{2,10},{3,11},{16,24},{17,25},{18,26},{19,27},{32,40},... | collective-permute-start | bytes 393224 | tf_op jit(solution)/shard_map/ppermute | solution.py:51
  21.9 24.8 %collective-permute-start.8 = (bf16[2,256,512]{2,1,0:T(8,128)(2,1)S(1)}, bf16[2,256,512]{2,1,0:T(8,128)(2,1)S(1)}, u32[]{:S(2)}, u32[]{:S(2)}) collective-permute-start(bf16[2,256,512]{2,1,0:T(8,128)(2,1)S(1)} %get-tuple-element.21), channel_id=1, source_target_pairs={{14,16},{15,17},{30,32},{31,33},{46,48},{47,49},{62,0},{63,1},{78,... | collective-permute-start | bytes 1572872 | tf_op jit(solution)/shard_map/ppermute | solution.py:51
  23.2 5.0 %collective-permute-start.5 = (bf16[256,128]{1,0:T(8,128)(2,1)S(1)}, bf16[256,128]{1,0:T(8,128)(2,1)S(1)}, u32[]{:S(2)}, u32[]{:S(2)}) collective-permute-start(bf16[256,128]{1,0:T(8,128)(2,1)S(1)} %slice.4), channel_id=1, source_target_pairs={{2,0},{3,1},{18,16},{19,17},{34,32},{35,33},{50,48},{51,49},{66,64... | collective-permute-start | bytes 196616 | tf_op jit(solution)/shard_map/ppermute | solution.py:51
  28.2 3.2 %collective-permute-start.6 = (bf16[512,128]{1,0:T(8,128)(2,1)S(1)}, bf16[512,128]{1,0:T(8,128)(2,1)S(1)}, u32[]{:S(2)}, u32[]{:S(2)}) collective-permute-start(bf16[512,128]{1,0:T(8,128)(2,1)S(1)} %broadcast_select_fusion.2), channel_id=1, source_target_pairs={{0,4},{1,5},{2,6},{3,7},{8,12},{9,13},{10,14},{11,15},{16,20},{17,... | collective-permute-start | bytes 393224 | tf_op jit(solution)/shard_map/ppermute | solution.py:51
  29.5 13.2 %collective-permute-start.10 = (bf16[256,512]{1,0:T(8,128)(2,1)S(1)}, bf16[256,512]{1,0:T(8,128)(2,1)S(1)}, u32[]{:S(2)}, u32[]{:S(2)}) collective-permute-start(bf16[256,512]{1,0:T(8,128)(2,1)S(1)} %get-tuple-element.24.odd), channel_id=1, source_target_pairs={{0,2},{1,3},{2,4},{3,5},{4,6},{5,7},{6,8},{7,9},{8,10},{9,11},{10,... | collective-permute-start | bytes 786440 | tf_op jit(solution)/shard_map/ppermute | solution.py:51
  31.5 14.5 %collective-permute-start.7 = (bf16[512,128]{1,0:T(8,128)(2,1)S(1)}, bf16[512,128]{1,0:T(8,128)(2,1)S(1)}, u32[]{:S(2)}, u32[]{:S(2)}) collective-permute-start(bf16[512,128]{1,0:T(8,128)(2,1)S(1)} %broadcast_select_fusion.3.held), channel_id=1, source_target_pairs={{0,2},{1,3},{2,4},{3,5},{4,6},{5,7},{6,8},{7,9},{8,10},{9,11},{10,... | collective-permute-start | bytes 393224 | tf_op jit(solution)/shard_map/ppermute | solution.py:51
  33.2 32.4 %collective-permute-start.13 = (bf16[2,256,512]{2,1,0:T(8,128)(2,1)S(1)}, bf16[2,256,512]{2,1,0:T(8,128)(2,1)S(1)}, u32[]{:S(2)}, u32[]{:S(2)}) collective-permute-start(bf16[2,256,512]{2,1,0:T(8,128)(2,1)S(1)} %shard_map.98), channel_id=1, source_target_pairs={{0,1},{1,0},{2,3},{3,2},{4,5},{5,4},{6,7},{7,6},{8,9},{9,8},{10,11... | collective-permute-start | bytes 1572872 | tf_op jit(solution)/shard_map/ppermute | solution.py:51
  41.4 24.1 %collective-permute-start.9 = (bf16[256,512]{1,0:T(8,128)(2,1)S(1)}, bf16[256,512]{1,0:T(8,128)(2,1)S(1)}, u32[]{:S(2)}, u32[]{:S(2)}) collective-permute-start(bf16[256,512]{1,0:T(8,128)(2,1)S(1)} %get-tuple-element.24.odd), channel_id=1, source_target_pairs={{12,16},{13,17},{14,18},{15,19},{28,32},{29,33},{30,34},{31,35},{4... | collective-permute-start | bytes 786440 | tf_op jit(solution)/shard_map/ppermute | solution.py:51
  42.7 22.8 %collective-permute-start.12 = (bf16[256,512]{1,0:T(8,128)(2,1)S(1)}, bf16[256,512]{1,0:T(8,128)(2,1)S(1)}, u32[]{:S(2)}, u32[]{:S(2)}) collective-permute-start(bf16[256,512]{1,0:T(8,128)(2,1)S(1)} %get-tuple-element.26.even), channel_id=1, source_target_pairs={{0,2},{1,3},{2,4},{3,5},{4,6},{5,7},{6,8},{7,9},{8,10},{9,11},{10,... | collective-permute-start | bytes 786440 | tf_op jit(solution)/shard_map/ppermute | solution.py:51
  46.0 19.6 %collective-permute-start.11 = (bf16[256,512]{1,0:T(8,128)(2,1)S(1)}, bf16[256,512]{1,0:T(8,128)(2,1)S(1)}, u32[]{:S(2)}, u32[]{:S(2)}) collective-permute-start(bf16[256,512]{1,0:T(8,128)(2,1)S(1)} %collective-permute-done.10.before_odd), channel_id=1, source_target_pairs={{2,4},{3,5},{4,6},{5,7},{6,8},{7,9},{8,10},{9,11},{10,12},{11,13},... | collective-permute-start | bytes 786440 | tf_op jit(solution)/shard_map/ppermute | solution.py:51
  46.7 18.9 %copy-start.4 = (bf16[1280,1280]{1,0:T(8,128)(2,1)S(1)}, bf16[1280,1280]{1,0:T(8,128)(2,1)}, u32[]{:S(2)}) copy-start(bf16[1280,1280]{1,0:T(8,128)(2,1)} %constant.70.clone.forward) | copy-start | bytes 9830404
  46.7 18.9 %copy-start.5 = (bf16[512,1280]{1,0:T(8,128)(2,1)S(1)}, bf16[512,1280]{1,0:T(8,128)(2,1)}, u32[]{:S(2)}) copy-start(bf16[512,1280]{1,0:T(8,128)(2,1)} %constant.71.clone.back) | copy-start | bytes 3932164
  65.6 22.8 %copy-start.7 = (bf16[1024]{0:T(1024)(128)(2,1)S(1)}, bf16[1024]{0:T(1024)(128)(2,1)}, u32[]{:S(2)}) copy-start(bf16[1024]{0:T(1024)(128)(2,1)} %param.13) | copy-start | bytes 6148
  70.4 30.6 %all-to-all-start = ((f32[16,1,256]{2,1,0:T(1,128)}), f32[16,1,256]{2,1,0:T(1,128)S(1)}, u32[]{:S(2)}, u32[]{:S(2)}) async-start(f32[16,1,256]{2,1,0:T(1,128)} %get-tuple-element.29), calls=%async_computation | async-start | bytes 32768 | tf_op jit(solution)/shard_map/all_to_all | solution.py:308
  86.4 14.5 %collective-permute-start.14 = (bf16[256,512]{1,0:T(8,128)(2,1)S(1)}, bf16[256,512]{1,0:T(8,128)(2,1)S(1)}, u32[]{:S(2)}, u32[]{:S(2)}) collective-permute-start(bf16[256,512]{1,0:T(8,128)(2,1)S(1)} %get-tuple-element.28), channel_id=1, source_target_pairs={{0,1},{1,0},{2,3},{3,2},{4,5},{5,4},{6,7},{7,6},{8,9},{9,8},{10,11... | collective-permute-start | bytes 786440 | tf_op jit(solution)/shard_map/ppermute | solution.py:51

commit v5 on v4

--- a/solution.py
+++ b/solution.py
@@ -262,7 +262,7 @@
     both, even, odd, *piece = prepare(flag(core), filter_taps, signal, other)
     parts = [
         move(piece[q], lambda y, z, c, q=q: (q, z, c) if y == 0 and z < 2 else None)
-        for q in (1, 3, 2)
+        for q in (1, 2, 3)
     ]
 
     before_odd = move(odd, lambda y, z, c: (y, z + 1, c) if z < Z - 1 else None)

time: 104 us -> 104 us (level)
  the two profiles are of different devices: /device:TPU:1 before, /device:TPU:33 now
where the time goes in v5:
time: 104 us
  starting transfers between devices  56.9 us (55%)
  blocking collectives  19.3 us (19%)
  waiting for transfers between devices  17.7 us (17%)
  Pallas kernels  5.08 us (5%)
  local copies, waits for them, and re-layouts  2.12 us (2%)
  other arithmetic  1.3 us (1%)
  between operations  1.07 us (1%)
    ppermute x15, starting transfers between devices, move(): return lax.ppermute(x, 'ctx', pairs(rule))  40.1 us
    all_gather x1, blocking collectives, local(): taps = lax.all_gather(quarter, 'ctx', axis_index_groups=groups)  19.3 us
    all_to_all x1, starting transfers between devices, local(): lax.all_to_all(sums, ('ch', 'ctx'), 0, 0, axis_index_groups=groups)  16.8 us
    all_to_all x1, waiting for transfers between devices, local(): lax.all_to_all(sums, ('ch', 'ctx'), 0, 0, axis_index_groups=groups)  12.5 us
    ppermute x15, waiting for transfers between devices, move(): return lax.ppermute(x, 'ctx', pairs(rule))  5.28 us
    pallas_call x1, Pallas kernels, mix(): pl.pallas_call(mix_kernel, out_shape=(shaped(BLOCK, HALF), shaped(BLOCK,...  4.75 us
    unnamed x16, local copies, waits for them, and re-layouts  2.11 us
  transfers between devices with their start and end apart: 16, of which 5 were waited for; matrix products, arithmetic and copies ran while one was open for 0% of the time, Pallas kernels for 0%

profile of v5, /device:TPU:33, one launch (start us, length us, event | category | flops | bytes accessed | tf_op | source)
XLA Modules:
  0.0 103.5 jit_solution(11732687301676118276)
XLA Ops:
  0.7 1.0 copy-done
  1.7 1.0 %copy-done.1 = bf16[256,1024]{1,0:T(8,128)(2,1)S(1)} copy-done((bf16[256,1024]{1,0:T(8,128)(2,1)S(1)}, bf16[256,1024]{1,0:T(8,128)(2,1)}, u32[]{:S(2)}) %copy-start.1) | copy-done | bytes 524312
  2.7 0.1 shard_map.95
  2.8 2.7 %collective-permute-start = (bf16[2,256,512]{2,1,0:T(8,128)(2,1)S(1)}, bf16[2,256,512]{2,1,0:T(8,128)(2,1)S(1)}, u32[]{:S(2)}, u32[]{:S(2)}) collective-permute-start(bf16[2,256,512]{2,1,0:T(8,128)(2,1)S(1)} %shard_map.95), channel_id=1, source_target_pairs={{0,1},{1,0},{2,3},{3,2},{4,5},{5,4},{6,7},{7,6},{8,9},{9,8},{10,11... | collective-permute-start | bytes 1572872 | tf_op jit(solution)/shard_map/ppermute | solution.py:51
  5.5 1.5 %collective-permute-done.other = bf16[2,256,512]{2,1,0:T(8,128)(2,1)S(1)} collective-permute-done((bf16[2,256,512]{2,1,0:T(8,128)(2,1)S(1)}, bf16[2,256,512]{2,1,0:T(8,128)(2,1)S(1)}, u32[]{:S(2)}, u32[]{:S(2)}) %collective-permute-start) | collective-permute-done | bytes 524320 | tf_op jit(solution)/shard_map/ppermute | solution.py:51
  7.0 0.2 shard_map.96
  7.2 3.2 %collective-permute-start.1 = (bf16[512,128]{1,0:T(8,128)(2,1)S(1)}, bf16[512,128]{1,0:T(8,128)(2,1)S(1)}, u32[]{:S(2)}, u32[]{:S(2)}) collective-permute-start(bf16[512,128]{1,0:T(8,128)(2,1)S(1)} %get-tuple-element.17), channel_id=1, source_target_pairs={{0,16},{1,17},{2,18},{3,19},{64,80},{65,81},{66,82},{67,83},{128,1... | collective-permute-start | bytes 393224 | tf_op jit(solution)/shard_map/ppermute | solution.py:51
  10.4 2.3 %collective-permute-start.2 = (bf16[512,128]{1,0:T(8,128)(2,1)S(1)}, bf16[512,128]{1,0:T(8,128)(2,1)S(1)}, u32[]{:S(2)}, u32[]{:S(2)}) collective-permute-start(bf16[512,128]{1,0:T(8,128)(2,1)S(1)} %get-tuple-element.18), channel_id=1, source_target_pairs={{0,32},{1,33},{2,34},{3,35},{64,96},{65,97},{66,98},{67,99},{128,1... | collective-permute-start | bytes 393224 | tf_op jit(solution)/shard_map/ppermute | solution.py:51
  12.7 1.3 %collective-permute-start.3 = (bf16[512,128]{1,0:T(8,128)(2,1)S(1)}, bf16[512,128]{1,0:T(8,128)(2,1)S(1)}, u32[]{:S(2)}, u32[]{:S(2)}) collective-permute-start(bf16[512,128]{1,0:T(8,128)(2,1)S(1)} %get-tuple-element.19), channel_id=1, source_target_pairs={{0,48},{1,49},{2,50},{3,51},{64,112},{65,113},{66,114},{67,115},{1... | collective-permute-start | bytes 393224 | tf_op jit(solution)/shard_map/ppermute | solution.py:51
  14.1 2.0 %collective-permute-done.2 = bf16[512,128]{1,0:T(8,128)(2,1)S(1)} collective-permute-done((bf16[512,128]{1,0:T(8,128)(2,1)S(1)}, bf16[512,128]{1,0:T(8,128)(2,1)S(1)}, u32[]{:S(2)}, u32[]{:S(2)}) %collective-permute-start.2) | collective-permute-done | bytes 131104 | tf_op jit(solution)/shard_map/ppermute | solution.py:51
  16.1 0.4 collective-permute-done.3
  16.6 1.6 %collective-permute-start.4 = (bf16[512,128]{1,0:T(8,128)(2,1)S(1)}, bf16[512,128]{1,0:T(8,128)(2,1)S(1)}, u32[]{:S(2)}, u32[]{:S(2)}) collective-permute-start(bf16[512,128]{1,0:T(8,128)(2,1)S(1)} %add_select_fusion), channel_id=1, source_target_pairs={{0,8},{1,9},{2,10},{3,11},{16,24},{17,25},{18,26},{19,27},{32,40},... | collective-permute-start | bytes 393224 | tf_op jit(solution)/shard_map/ppermute | solution.py:51
  18.2 0.7 collective-permute-start.8
  18.9 5.0 %collective-permute-start.5 = (bf16[256,128]{1,0:T(8,128)(2,1)S(1)}, bf16[256,128]{1,0:T(8,128)(2,1)S(1)}, u32[]{:S(2)}, u32[]{:S(2)}) collective-permute-start(bf16[256,128]{1,0:T(8,128)(2,1)S(1)} %slice.4), channel_id=1, source_target_pairs={{2,0},{3,1},{18,16},{19,17},{34,32},{35,33},{50,48},{51,49},{66,64... | collective-permute-start | bytes 196616 | tf_op jit(solution)/shard_map/ppermute | solution.py:51
  24.0 1.3 %collective-permute-done.5.extra = bf16[256,128]{1,0:T(8,128)(2,1)S(1)} collective-permute-done((bf16[256,128]{1,0:T(8,128)(2,1)S(1)}, bf16[256,128]{1,0:T(8,128)(2,1)S(1)}, u32[]{:S(2)}, u32[]{:S(2)}) %collective-permute-start.5) | collective-permute-done | bytes 65568 | tf_op jit(solution)/shard_map/ppermute | solution.py:51
  25.3 1.3 %collective-permute-start.6 = (bf16[512,128]{1,0:T(8,128)(2,1)S(1)}, bf16[512,128]{1,0:T(8,128)(2,1)S(1)}, u32[]{:S(2)}, u32[]{:S(2)}) collective-permute-start(bf16[512,128]{1,0:T(8,128)(2,1)S(1)} %broadcast_select_fusion.2), channel_id=1, source_target_pairs={{0,4},{1,5},{2,6},{3,7},{8,12},{9,13},{10,14},{11,15},{16,20},{17,... | collective-permute-start | bytes 393224 | tf_op jit(solution)/shard_map/ppermute | solution.py:51
  26.6 1.9 %collective-permute-start.10 = (bf16[256,512]{1,0:T(8,128)(2,1)S(1)}, bf16[256,512]{1,0:T(8,128)(2,1)S(1)}, u32[]{:S(2)}, u32[]{:S(2)}) collective-permute-start(bf16[256,512]{1,0:T(8,128)(2,1)S(1)} %get-tuple-element.24.odd), channel_id=1, source_target_pairs={{0,2},{1,3},{2,4},{3,5},{4,6},{5,7},{6,8},{7,9},{8,10},{9,11},{10,... | collective-permute-start | bytes 786440 | tf_op jit(solution)/shard_map/ppermute | solution.py:51
  28.5 5.3 %collective-permute-start.7 = (bf16[512,128]{1,0:T(8,128)(2,1)S(1)}, bf16[512,128]{1,0:T(8,128)(2,1)S(1)}, u32[]{:S(2)}, u32[]{:S(2)}) collective-permute-start(bf16[512,128]{1,0:T(8,128)(2,1)S(1)} %broadcast_select_fusion.3.held), channel_id=1, source_target_pairs={{0,2},{1,3},{2,4},{3,5},{4,6},{5,7},{6,8},{7,9},{8,10},{9,11},{10,... | collective-permute-start | bytes 393224 | tf_op jit(solution)/shard_map/ppermute | solution.py:51
  33.9 0.1 shard_map.98
  34.0 6.3 %collective-permute-start.13 = (bf16[2,256,512]{2,1,0:T(8,128)(2,1)S(1)}, bf16[2,256,512]{2,1,0:T(8,128)(2,1)S(1)}, u32[]{:S(2)}, u32[]{:S(2)}) collective-permute-start(bf16[2,256,512]{2,1,0:T(8,128)(2,1)S(1)} %shard_map.98), channel_id=1, source_target_pairs={{0,1},{1,0},{2,3},{3,2},{4,5},{5,4},{6,7},{7,6},{8,9},{9,8},{10,11... | collective-permute-start | bytes 1572872 | tf_op jit(solution)/shard_map/ppermute | solution.py:51
  40.3 1.3 %collective-permute-start.9 = (bf16[256,512]{1,0:T(8,128)(2,1)S(1)}, bf16[256,512]{1,0:T(8,128)(2,1)S(1)}, u32[]{:S(2)}, u32[]{:S(2)}) collective-permute-start(bf16[256,512]{1,0:T(8,128)(2,1)S(1)} %get-tuple-element.24.odd), channel_id=1, source_target_pairs={{12,16},{13,17},{14,18},{15,19},{28,32},{29,33},{30,34},{31,35},{4... | collective-permute-start | bytes 786440 | tf_op jit(solution)/shard_map/ppermute | solution.py:51
  41.6 3.1 %collective-permute-start.12 = (bf16[256,512]{1,0:T(8,128)(2,1)S(1)}, bf16[256,512]{1,0:T(8,128)(2,1)S(1)}, u32[]{:S(2)}, u32[]{:S(2)}) collective-permute-start(bf16[256,512]{1,0:T(8,128)(2,1)S(1)} %get-tuple-element.26.even), channel_id=1, source_target_pairs={{0,2},{1,3},{2,4},{3,5},{4,6},{5,7},{6,8},{7,9},{8,10},{9,11},{10,... | collective-permute-start | bytes 786440 | tf_op jit(solution)/shard_map/ppermute | solution.py:51
  44.8 1.9 %collective-permute-start.11 = (bf16[256,512]{1,0:T(8,128)(2,1)S(1)}, bf16[256,512]{1,0:T(8,128)(2,1)S(1)}, u32[]{:S(2)}, u32[]{:S(2)}) collective-permute-start(bf16[256,512]{1,0:T(8,128)(2,1)S(1)} %collective-permute-done.10.before_odd), channel_id=1, source_target_pairs={{2,4},{3,5},{4,6},{5,7},{6,8},{7,9},{8,10},{9,11},{10,12},{11,13},... | collective-permute-start | bytes 786440 | tf_op jit(solution)/shard_map/ppermute | solution.py:51
  46.7 0.0 copy-start.4
  46.8 0.0 copy-start.5
  46.8 19.3 %all-gather = bf16[3072,128]{1,0:T(8,128)(2,1)S(1)} all-gather(bf16[768,128]{1,0:T(8,128)(2,1)S(1)} %shard_map.97), channel_id=2, replica_groups={{0,16,32,48},{1,17,33,49},{2,18,34,50},{3,19,35,51},{4,20,36,52},{5,21,..., dimensions={0}, use_global_device_ids=true | all-gather | bytes 983040 | tf_op jit(solution)/shard_map/all_gather | solution.py:285
  66.2 0.0 copy-start.7
  66.2 4.7 %shard_map.99 = (bf16[256,512]{1,0:T(8,128)(2,1)S(1)}, bf16[256,512]{1,0:T(8,128)(2,1)S(1)}, f32[16,1,256]{2,1,0:T(1,128)}) custom-call(s32[1]{0:T(128)} %bitcast.core, s32[1]{0:T(128)} %bitcast.1.place, bf16[1280,1280]{1,0:T(8,128)(2,1)S(1)} %copy-done.4, bf16[512,1280]{1,0:T(8,128)(2,1)S(1)} %copy-done.5, bf16[4,768,128]{2,1,0:T(8,128)(2,1)S(1)} %bitcast.3, ...), custom_call_target="tpu_custom_call" | custom-call | flops 3355443200 | bytes 4587520 | tf_op jit(solution)/shard_map/pallas_call | solution.py:230
  71.0 16.8 %all-to-all-start = ((f32[16,1,256]{2,1,0:T(1,128)}), f32[16,1,256]{2,1,0:T(1,128)S(1)}, u32[]{:S(2)}, u32[]{:S(2)}) async-start(f32[16,1,256]{2,1,0:T(1,128)} %get-tuple-element.29), calls=%async_computation | async-start | bytes 32768 | tf_op jit(solution)/shard_map/all_to_all | solution.py:308
  87.8 2.0 %collective-permute-start.14 = (bf16[256,512]{1,0:T(8,128)(2,1)S(1)}, bf16[256,512]{1,0:T(8,128)(2,1)S(1)}, u32[]{:S(2)}, u32[]{:S(2)}) collective-permute-start(bf16[256,512]{1,0:T(8,128)(2,1)S(1)} %get-tuple-element.28), channel_id=1, source_target_pairs={{0,1},{1,0},{2,3},{3,2},{4,5},{5,4},{6,7},{7,6},{8,9},{9,8},{10,11... | collective-permute-start | bytes 786440 | tf_op jit(solution)/shard_map/ppermute | solution.py:51
  89.8 12.5 %all-to-all-done = f32[16,1,256]{2,1,0:T(1,128)S(1)} async-done(((f32[16,1,256]{2,1,0:T(1,128)}), f32[16,1,256]{2,1,0:T(1,128)S(1)}, u32[]{:S(2)}, u32[]{:S(2)}) %all-to-all-start) | async-done | bytes 16416 | tf_op jit(solution)/shard_map/all_to_all | solution.py:308
  102.4 1.1 %multiply_convert_fusion = (bf16[256,1024]{1,0:T(8,128)(2,1)}, bf16[256,1024]{1,0:T(8,128)(2,1)}) fusion(f32[1024]{0:T(1024)S(1)} %convert_element_type.10, f32[256]{0:T(256)S(1)} %add_rsqrt_fusion, bf16[256,512]{1,0:T(8,128)(2,1)S(1)} %get-tuple-element.33, bf16[256,512]{1,0:T(8,128)(2,1)S(1)} %get-tuple-element.32), kind=kLoop, calls=%fused_computation | loop fusion | flops 2097152 | bytes 1577984 | tf_op jit(solution)/shard_map/convert_element_type | solution.py:316
  (32 shorter events, 0.3 us)
Async XLA Ops:
  0.6 39.7 %copy-start.6 = (bf16[1024]{0:T(1024)(128)(2,1)S(1)}, bf16[1024]{0:T(1024)(128)(2,1)}, u32[]{:S(2)}) copy-start(bf16[1024]{0:T(1024)(128)(2,1)} %param.11) | copy-start | bytes 6148
  0.7 1.0 %copy-start = (bf16[256,1024]{1,0:T(8,128)(2,1)S(1)}, bf16[256,1024]{1,0:T(8,128)(2,1)}, u32[]{:S(2)}) copy-start(bf16[256,1024]{1,0:T(8,128)(2,1)} %taps.1) | copy-start | bytes 1572868
  1.7 1.0 %copy-start.1 = (bf16[256,1024]{1,0:T(8,128)(2,1)S(1)}, bf16[256,1024]{1,0:T(8,128)(2,1)}, u32[]{:S(2)}) copy-start(bf16[256,1024]{1,0:T(8,128)(2,1)} %signal.1) | copy-start | bytes 1572868
  2.7 31.1 %copy-start.2 = (bf16[256,1024]{1,0:T(8,128)(2,1)S(1)}, bf16[256,1024]{1,0:T(8,128)(2,1)}, u32[]{:S(2)}) copy-start(bf16[256,1024]{1,0:T(8,128)(2,1)} %gate.1) | copy-start | bytes 1572868
  2.7 31.1 %copy-start.3 = (bf16[256,1024]{1,0:T(8,128)(2,1)S(1)}, bf16[256,1024]{1,0:T(8,128)(2,1)}, u32[]{:S(2)}) copy-start(bf16[256,1024]{1,0:T(8,128)(2,1)} %residual.1) | copy-start | bytes 1572868
  2.8 4.2 %collective-permute-start = (bf16[2,256,512]{2,1,0:T(8,128)(2,1)S(1)}, bf16[2,256,512]{2,1,0:T(8,128)(2,1)S(1)}, u32[]{:S(2)}, u32[]{:S(2)}) collective-permute-start(bf16[2,256,512]{2,1,0:T(8,128)(2,1)S(1)} %shard_map.95), channel_id=1, source_target_pairs={{0,1},{1,0},{2,3},{3,2},{4,5},{5,4},{6,7},{7,6},{8,9},{9,8},{10,11... | collective-permute-start | bytes 1572872 | tf_op jit(solution)/shard_map/ppermute | solution.py:51
  7.2 6.8 %collective-permute-start.1 = (bf16[512,128]{1,0:T(8,128)(2,1)S(1)}, bf16[512,128]{1,0:T(8,128)(2,1)S(1)}, u32[]{:S(2)}, u32[]{:S(2)}) collective-permute-start(bf16[512,128]{1,0:T(8,128)(2,1)S(1)} %get-tuple-element.17), channel_id=1, source_target_pairs={{0,16},{1,17},{2,18},{3,19},{64,80},{65,81},{66,82},{67,83},{128,1... | collective-permute-start | bytes 393224 | tf_op jit(solution)/shard_map/ppermute | solution.py:51
  10.4 5.6 %collective-permute-start.2 = (bf16[512,128]{1,0:T(8,128)(2,1)S(1)}, bf16[512,128]{1,0:T(8,128)(2,1)S(1)}, u32[]{:S(2)}, u32[]{:S(2)}) collective-permute-start(bf16[512,128]{1,0:T(8,128)(2,1)S(1)} %get-tuple-element.18), channel_id=1, source_target_pairs={{0,32},{1,33},{2,34},{3,35},{64,96},{65,97},{66,98},{67,99},{128,1... | collective-permute-start | bytes 393224 | tf_op jit(solution)/shard_map/ppermute | solution.py:51
  12.7 3.8 %collective-permute-start.3 = (bf16[512,128]{1,0:T(8,128)(2,1)S(1)}, bf16[512,128]{1,0:T(8,128)(2,1)S(1)}, u32[]{:S(2)}, u32[]{:S(2)}) collective-permute-start(bf16[512,128]{1,0:T(8,128)(2,1)S(1)} %get-tuple-element.19), channel_id=1, source_target_pairs={{0,48},{1,49},{2,50},{3,51},{64,112},{65,113},{66,114},{67,115},{1... | collective-permute-start | bytes 393224 | tf_op jit(solution)/shard_map/ppermute | solution.py:51
  16.6 7.4 %collective-permute-start.4 = (bf16[512,128]{1,0:T(8,128)(2,1)S(1)}, bf16[512,128]{1,0:T(8,128)(2,1)S(1)}, u32[]{:S(2)}, u32[]{:S(2)}) collective-permute-start(bf16[512,128]{1,0:T(8,128)(2,1)S(1)} %add_select_fusion), channel_id=1, source_target_pairs={{0,8},{1,9},{2,10},{3,11},{16,24},{17,25},{18,26},{19,27},{32,40},... | collective-permute-start | bytes 393224 | tf_op jit(solution)/shard_map/ppermute | solution.py:51
  18.2 28.5 %collective-permute-start.8 = (bf16[2,256,512]{2,1,0:T(8,128)(2,1)S(1)}, bf16[2,256,512]{2,1,0:T(8,128)(2,1)S(1)}, u32[]{:S(2)}, u32[]{:S(2)}) collective-permute-start(bf16[2,256,512]{2,1,0:T(8,128)(2,1)S(1)} %get-tuple-element.21), channel_id=1, source_target_pairs={{14,16},{15,17},{30,32},{31,33},{46,48},{47,49},{62,0},{63,1},{78,... | collective-permute-start | bytes 1572872 | tf_op jit(solution)/shard_map/ppermute | solution.py:51
  18.9 6.3 %collective-permute-start.5 = (bf16[256,128]{1,0:T(8,128)(2,1)S(1)}, bf16[256,128]{1,0:T(8,128)(2,1)S(1)}, u32[]{:S(2)}, u32[]{:S(2)}) collective-permute-start(bf16[256,128]{1,0:T(8,128)(2,1)S(1)} %slice.4), channel_id=1, source_target_pairs={{2,0},{3,1},{18,16},{19,17},{34,32},{35,33},{50,48},{51,49},{66,64... | collective-permute-start | bytes 196616 | tf_op jit(solution)/shard_map/ppermute | solution.py:51
  25.3 3.2 %collective-permute-start.6 = (bf16[512,128]{1,0:T(8,128)(2,1)S(1)}, bf16[512,128]{1,0:T(8,128)(2,1)S(1)}, u32[]{:S(2)}, u32[]{:S(2)}) collective-permute-start(bf16[512,128]{1,0:T(8,128)(2,1)S(1)} %broadcast_select_fusion.2), channel_id=1, source_target_pairs={{0,4},{1,5},{2,6},{3,7},{8,12},{9,13},{10,14},{11,15},{16,20},{17,... | collective-permute-start | bytes 393224 | tf_op jit(solution)/shard_map/ppermute | solution.py:51
  26.6 15.1 %collective-permute-start.10 = (bf16[256,512]{1,0:T(8,128)(2,1)S(1)}, bf16[256,512]{1,0:T(8,128)(2,1)S(1)}, u32[]{:S(2)}, u32[]{:S(2)}) collective-permute-start(bf16[256,512]{1,0:T(8,128)(2,1)S(1)} %get-tuple-element.24.odd), channel_id=1, source_target_pairs={{0,2},{1,3},{2,4},{3,5},{4,6},{5,7},{6,8},{7,9},{8,10},{9,11},{10,... | collective-permute-start | bytes 786440 | tf_op jit(solution)/shard_map/ppermute | solution.py:51
  28.5 16.3 %collective-permute-start.7 = (bf16[512,128]{1,0:T(8,128)(2,1)S(1)}, bf16[512,128]{1,0:T(8,128)(2,1)S(1)}, u32[]{:S(2)}, u32[]{:S(2)}) collective-permute-start(bf16[512,128]{1,0:T(8,128)(2,1)S(1)} %broadcast_select_fusion.3.held), channel_id=1, source_target_pairs={{0,2},{1,3},{2,4},{3,5},{4,6},{5,7},{6,8},{7,9},{8,10},{9,11},{10,... | collective-permute-start | bytes 393224 | tf_op jit(solution)/shard_map/ppermute | solution.py:51
  34.0 32.2 %collective-permute-start.13 = (bf16[2,256,512]{2,1,0:T(8,128)(2,1)S(1)}, bf16[2,256,512]{2,1,0:T(8,128)(2,1)S(1)}, u32[]{:S(2)}, u32[]{:S(2)}) collective-permute-start(bf16[2,256,512]{2,1,0:T(8,128)(2,1)S(1)} %shard_map.98), channel_id=1, source_target_pairs={{0,1},{1,0},{2,3},{3,2},{4,5},{5,4},{6,7},{7,6},{8,9},{9,8},{10,11... | collective-permute-start | bytes 1572872 | tf_op jit(solution)/shard_map/ppermute | solution.py:51
  40.3 25.8 %collective-permute-start.9 = (bf16[256,512]{1,0:T(8,128)(2,1)S(1)}, bf16[256,512]{1,0:T(8,128)(2,1)S(1)}, u32[]{:S(2)}, u32[]{:S(2)}) collective-permute-start(bf16[256,512]{1,0:T(8,128)(2,1)S(1)} %get-tuple-element.24.odd), channel_id=1, source_target_pairs={{12,16},{13,17},{14,18},{15,19},{28,32},{29,33},{30,34},{31,35},{4... | collective-permute-start | bytes 786440 | tf_op jit(solution)/shard_map/ppermute | solution.py:51
  41.6 24.5 %collective-permute-start.12 = (bf16[256,512]{1,0:T(8,128)(2,1)S(1)}, bf16[256,512]{1,0:T(8,128)(2,1)S(1)}, u32[]{:S(2)}, u32[]{:S(2)}) collective-permute-start(bf16[256,512]{1,0:T(8,128)(2,1)S(1)} %get-tuple-element.26.even), channel_id=1, source_target_pairs={{0,2},{1,3},{2,4},{3,5},{4,6},{5,7},{6,8},{7,9},{8,10},{9,11},{10,... | collective-permute-start | bytes 786440 | tf_op jit(solution)/shard_map/ppermute | solution.py:51
  44.8 21.4 %collective-permute-start.11 = (bf16[256,512]{1,0:T(8,128)(2,1)S(1)}, bf16[256,512]{1,0:T(8,128)(2,1)S(1)}, u32[]{:S(2)}, u32[]{:S(2)}) collective-permute-start(bf16[256,512]{1,0:T(8,128)(2,1)S(1)} %collective-permute-done.10.before_odd), channel_id=1, source_target_pairs={{2,4},{3,5},{4,6},{5,7},{6,8},{7,9},{8,10},{9,11},{10,12},{11,13},... | collective-permute-start | bytes 786440 | tf_op jit(solution)/shard_map/ppermute | solution.py:51
  46.7 19.4 %copy-start.4 = (bf16[1280,1280]{1,0:T(8,128)(2,1)S(1)}, bf16[1280,1280]{1,0:T(8,128)(2,1)}, u32[]{:S(2)}) copy-start(bf16[1280,1280]{1,0:T(8,128)(2,1)} %constant.70.clone.forward) | copy-start | bytes 9830404
  46.8 19.4 %copy-start.5 = (bf16[512,1280]{1,0:T(8,128)(2,1)S(1)}, bf16[512,1280]{1,0:T(8,128)(2,1)}, u32[]{:S(2)}) copy-start(bf16[512,1280]{1,0:T(8,128)(2,1)} %constant.71.clone.back) | copy-start | bytes 3932164
  66.2 23.6 %copy-start.7 = (bf16[1024]{0:T(1024)(128)(2,1)S(1)}, bf16[1024]{0:T(1024)(128)(2,1)}, u32[]{:S(2)}) copy-start(bf16[1024]{0:T(1024)(128)(2,1)} %param.13) | copy-start | bytes 6148
  71.0 31.3 %all-to-all-start = ((f32[16,1,256]{2,1,0:T(1,128)}), f32[16,1,256]{2,1,0:T(1,128)S(1)}, u32[]{:S(2)}, u32[]{:S(2)}) async-start(f32[16,1,256]{2,1,0:T(1,128)} %get-tuple-element.29), calls=%async_computation | async-start | bytes 32768 | tf_op jit(solution)/shard_map/all_to_all | solution.py:308
  87.8 14.5 %collective-permute-start.14 = (bf16[256,512]{1,0:T(8,128)(2,1)S(1)}, bf16[256,512]{1,0:T(8,128)(2,1)S(1)}, u32[]{:S(2)}, u32[]{:S(2)}) collective-permute-start(bf16[256,512]{1,0:T(8,128)(2,1)S(1)} %get-tuple-element.28), channel_id=1, source_target_pairs={{0,1},{1,0},{2,3},{3,2},{4,5},{5,4},{6,7},{7,6},{8,9},{9,8},{10,11... | collective-permute-start | bytes 786440 | tf_op jit(solution)/shard_map/ppermute | solution.py:51
